TPU v7x, 128 devices: a whole 4x4x4 slice. The times are simulated.
128 devices in a mesh: store: 4 (over z), ctx: 16 (over y, x), head: 2 (over core).
Axes of the slice: x: 4, y: 4, z: 4, core: 2. Of those that a mesh axis runs over, the one named last changes fastest.
Arguments:
- queries: bfloat16 [512, 64, 128], P(('store', 'ctx', 'head')), may hold values from -12 to 12
- suffix_k: bfloat16 [512, 8, 128], P(('store', 'ctx'), 'head'), may hold values from -6 to 6
- suffix_v: bfloat16 [512, 8, 128], P(('store', 'ctx'), 'head'), may hold values from -6 to 6
- pool_k: bfloat16 [1024, 256, 8, 128], P(('store', 'ctx'), None, 'head'), may hold values from -6 to 6
- pool_v: bfloat16 [1024, 256, 8, 128], P(('store', 'ctx'), None, 'head'), may hold values from -6 to 6
- list_holder: int32 [512, 1], P(('store', 'ctx')), may hold values from 0 to 3; in each aligned block of 8 rows (0 to 7, 8 to 15, ...) at most 3 rows name the same one
- list_slot: int32 [512], P(('store', 'ctx')), may hold values from 0 to 15
- list_valid: int32 [512], P(('store', 'ctx')), may hold values from 0 to 256, as said below
Outputs:
- mixed: bfloat16 [512, 64, 128], P(('store', 'ctx', 'head'))
Inputs may be any that keep to these rules, and one draw needn't show every extreme that they name: `list_holder`: at most 3 of the 8 entries of one index of store+ctx name the same store index. `list_valid`: 0 marks a padding entry; each index of store+ctx has at least one full block among its 8 entries.
All inputs are finite; a program needn't handle non-finite values.
Results may differ from a plain program's by a relative error of at most 0.0016.
Values may be sent and summed in bfloat16 or wider, within the bound.
A program may use at most 128 MiB of HBM per device.

v0:
```python
import math

import jax
import jax.numpy as jnp
from jax import lax
from jax.sharding import PartitionSpec as P

NEG_FILL = -1e30


def block_terms(query_all, key_tile, value_tile, live_mask):
    query_rows, head_count, head_width = query_all.shape
    kv_count = key_tile.shape[1]
    grouped = query_all.reshape(query_rows, kv_count, head_count // kv_count, head_width)
    scores = jnp.einsum(
        "rgqd,kgd->rgqk", grouped, key_tile, preferred_element_type=jnp.float32
    ) / math.sqrt(head_width)
    live_wide = live_mask[:, None, None, :]
    masked = jnp.where(live_wide, scores, NEG_FILL)
    block_peak = jnp.max(masked, axis=3)
    weights = jnp.where(live_wide, jnp.exp(masked - block_peak[..., None]), 0.0).astype(
        jnp.bfloat16
    )
    total_sum = jnp.sum(weights.astype(jnp.float32), axis=3)
    weighted = jnp.einsum("rgqk,kgd->rgqd", weights, value_tile, preferred_element_type=jnp.float32)
    return (
        block_peak.reshape(query_rows, head_count),
        total_sum.reshape(query_rows, head_count),
        weighted.reshape(query_rows, head_count, head_width),
    )


def merge_terms(carried, incoming):
    peak_old, total_old, weighted_old = carried
    peak_new, total_new, weighted_new = incoming
    joined = jnp.maximum(peak_old, peak_new)
    factor_old = jnp.exp(peak_old - joined)
    factor_new = jnp.exp(peak_new - joined)
    return (
        joined,
        total_old * factor_old + total_new * factor_new,
        weighted_old * factor_old[..., None] + weighted_new * factor_new[..., None],
    )


def fold_blocks(query_all, keys_many, values_many, valid_many, carried):
    positions = jnp.arange(keys_many.shape[1], dtype=jnp.int32)
    query_rows = query_all.shape[0]

    def advance(state, element):
        key_tile, value_tile, valid_count = element
        live_mask = jnp.broadcast_to(
            positions[None, :] < valid_count, (query_rows, positions.shape[0])
        )
        return (merge_terms(state, block_terms(query_all, key_tile, value_tile, live_mask)), None)

    result, _unused = lax.scan(advance, carried, (keys_many, values_many, valid_many))
    return result


def local(queries, suffix_k, suffix_v, pool_k, pool_v, list_holder, list_slot, list_valid):
    store_count = lax.axis_size("store")
    owned = lax.all_to_all(queries, "head", split_axis=1, concat_axis=0, tiled=True)
    every_query = lax.all_gather(owned, ("store", "ctx"), axis=0, tiled=True)
    query_rows, head_count, head_width = every_query.shape
    holder = list_holder[:, 0]
    entry_count = holder.shape[0]
    most_count = max(2, 3 * entry_count // (2 * store_count))
    order = jnp.arange(entry_count, dtype=jnp.int32)
    earlier_same = (holder[:, None] == holder[None, :]) & (order[None, :] < order[:, None])
    rank_within = jnp.sum(earlier_same.astype(jnp.int32), axis=1)
    placement_index = holder * most_count + rank_within
    cell_index = jnp.arange(store_count * most_count, dtype=jnp.int32)
    one_hot = (placement_index[:, None] == cell_index[None, :]).astype(jnp.int32)
    wanted_slot = jnp.sum(one_hot * list_slot[:, None], axis=0)
    wanted_valid = jnp.sum(one_hot * list_valid[:, None], axis=0)
    asked_slot, asked_valid = (
        lax.all_to_all(wanted_slot, "store", split_axis=0, concat_axis=0, tiled=True),
        lax.all_to_all(wanted_valid, "store", split_axis=0, concat_axis=0, tiled=True),
    )
    start_state = (
        jnp.full((query_rows, head_count), NEG_FILL, jnp.float32),
        jnp.zeros((query_rows, head_count), jnp.float32),
        jnp.zeros((query_rows, head_count, head_width), jnp.float32),
    )
    sent_keys = jnp.take(pool_k, asked_slot, axis=0)
    sent_values = jnp.take(pool_v, asked_slot, axis=0)
    got_keys, got_values = (
        lax.all_to_all(sent_keys, "store", split_axis=0, concat_axis=0, tiled=True),
        lax.all_to_all(sent_values, "store", split_axis=0, concat_axis=0, tiled=True),
    )
    picked_keys = jnp.take(got_keys, placement_index, axis=0)
    picked_values = jnp.take(got_values, placement_index, axis=0)
    carried = fold_blocks(every_query, picked_keys, picked_values, list_valid, start_state)
    group_size = suffix_k.shape[0]
    where_index = lax.axis_index(("store", "ctx"))
    key_index = where_index * group_size + jnp.arange(group_size, dtype=jnp.int32)
    query_index = jnp.arange(query_rows, dtype=jnp.int32)
    suffix_live = key_index[None, :] <= query_index[:, None]
    carried = merge_terms(carried, block_terms(every_query, suffix_k, suffix_v, suffix_live))
    local_peak, local_total, local_weighted = carried
    global_peak = lax.pmax(local_peak.astype(jnp.bfloat16), ("store", "ctx")).astype(
        local_peak.dtype
    )
    factor = jnp.exp(local_peak - global_peak)
    summed_values, summed_totals = (
        lax.psum_scatter(
            local_weighted * factor[..., None], ("store", "ctx"), scatter_dimension=0, tiled=True
        ),
        lax.psum_scatter(local_total * factor, ("store", "ctx"), scatter_dimension=0, tiled=True),
    )
    mixed_group = (summed_values / summed_totals[..., None]).astype(jnp.bfloat16)
    return lax.all_to_all(mixed_group, "head", split_axis=0, concat_axis=1, tiled=True)


def solution(mesh):
    in_specs = (
        P(("store", "ctx", "head"), None, None),
        P(("store", "ctx"), "head", None),
        P(("store", "ctx"), "head", None),
        P(("store", "ctx"), None, "head", None),
        P(("store", "ctx"), None, "head", None),
        P(("store", "ctx"), None),
        P(("store", "ctx")),
        P(("store", "ctx")),
    )
    out_specs = P(("store", "ctx", "head"), None, None)
    return jax.shard_map(local, mesh=mesh, in_specs=in_specs, out_specs=out_specs, check_vma=False)
```

profile of v0, /device:TPU:1, one launch (start us, length us, event | category | flops | bytes accessed | tf_op | source)
XLA Modules:
  0.0 1248.5 jit_solution(14838341388617533371)
XLA Ops:
  15.4 9.0 all_to_all.59
  25.8 7.7 gather_fusion
  33.5 7.3 gather_fusion.2
  40.9 6.9 broadcast_select_fusion
  47.8 50.6 %all_to_all.60 = bf16[12,256,4,128]{3,2,1,0:T(4,128)(2,1)} all-to-all(bf16[12,256,4,128]{3,2,1,0:T(4,128)(2,1)S(1)} %get-tuple-element.153), channel_id=1, replica_groups=mesh['store'=4,'ctx'=16,'head'=2] {'store'}, dimensions={0} | all-to-all | bytes 6291456 | tf_op jit(solution)/shard_map/all_to_all | solution.py:89
  111.2 30.8 %all-to-all-done.3 = bf16[12,256,4,128]{3,2,1,0:T(4,128)(2,1)S(1)} async-done(((bf16[12,256,4,128]{3,2,1,0:T(4,128)(2,1)}), bf16[12,256,4,128]{3,2,1,0:T(4,128)(2,1)S(1)}, u32[]{:S(2)}, u32[]{:S(2)}) %all-to-all-start.3) | async-done | bytes 3145760 | tf_op jit(solution)/shard_map/all_to_all | solution.py:90
  152.9 231.2 %while.15 = (s32[]{:T(128)}, f32[512,32]{0,1:T(8,128)S(1)}, f32[512,32]{0,1:T(8,128)S(1)}, f32[512,32,128]{0,2,1:T(8,128)}, s32[8]{0:T(128)S(1)}, /*index=5*/bf1...) while((s32[]{:T(128)}, f32[512,32]{0,1:T(8,128)S(1)}, ...), condition=%wide.region_5.8_spmd.clone, body=%wide.region_2.7_spmd.clone.sunk | while | flops 2197913856 | bytes 89458552 | solution.py:57
  158.8 5.8 convert_reduce_fusion.4
  164.6 5.5 fusion.47
  170.2 9.5 fusion.48
  185.6 5.8 convert_reduce_fusion.4
  191.5 5.5 fusion.47
  197.0 11.9 fusion.48
  214.8 5.8 convert_reduce_fusion.4
  226.2 11.9 fusion.48
  244.0 5.8 convert_reduce_fusion.4
  255.4 11.9 fusion.48
  273.2 5.8 convert_reduce_fusion.4
  284.6 11.9 fusion.48
  302.4 5.8 convert_reduce_fusion.4
  313.8 11.9 fusion.48
  331.6 5.8 convert_reduce_fusion.4
  343.0 11.9 fusion.48
  360.8 5.8 convert_reduce_fusion.4
  366.6 5.5 fusion.47
  372.2 11.9 fusion.48
  387.5 292.4 %pmax.7 = bf16[512,32]{0,1:T(8,128)(2,1)S(1)} all-reduce(bf16[512,32]{0,1:T(8,128)(2,1)S(1)} %fusion.23), channel_id=1, replica_groups=mesh['store'=4,'ctx'=16,'head'=2] {'store','ctx'}, use_global_device_ids=true, to_apply=%region_7.10 | all-reduce | flops 16384 | bytes 65536 | tf_op jit(solution)/shard_map/pmax | solution.py:102
  681.2 10.3 copy.65
  696.4 10.4 fusion.17
  708.5 157.9 %all-reduce.3.cloned.1.call-done = f32[512,32]{0,1:T(8,128)} async-done(((f32[512,32]{0,1:T(8,128)}), f32[512,32]{0,1:T(8,128)}) %all-reduce.3.cloned.1.call-update) | async-done | bytes 65552
  867.3 323.6 %reduce-scatter.3.cloned.1.call-done = f32[8,32,128]{2,1,0:T(8,128)} async-done(((f32[512,32,128]{2,1,0:T(8,128)}), f32[8,32,128]{2,1,0:T(8,128)}) %reduce-scatter.3.cloned.1.call-update) | async-done | bytes 131088 | tf_op jit(solution)/shard_map/reduce_scatter | solution.py:107
  1191.8 49.5 %all_to_all.61 = bf16[8,32,128]{2,1,0:T(8,128)(2,1)S(1)} all-to-all(bf16[8,32,128]{2,1,0:T(8,128)(2,1)S(1)} %divide_convert_fusion), channel_id=1, replica_groups=mesh['store'=4,'ctx'=16,'head'=2] {'head'}, dimensions={0} | all-to-all | bytes 131072 | tf_op jit(solution)/shard_map/all_to_all | solution.py:113
  (95 shorter events, 122.2 us)
Async XLA Ops:
  6.5 685.0 %copy-start = (bf16[8,4,128]{2,1,0:T(4,128)(2,1)S(1)}, bf16[8,4,128]{2,1,0:T(4,128)(2,1)}, u32[]{:S(2)}) copy-start(bf16[8,4,128]{2,1,0:T(4,128)(2,1)} %param.16) | copy-start | bytes 24580
  6.5 146.4 %all-gather.2.cloned.1.call-start = ((), (), s32[]{:S(2)}) async-start(), calls=%async_computation.6 | async-start | bytes 4259840 | tf_op jit(solution)/shard_map/all_gather | solution.py:64
  98.3 4.1 copy-start.3
  98.3 43.7 %all-to-all-start.3 = ((bf16[12,256,4,128]{3,2,1,0:T(4,128)(2,1)}), bf16[12,256,4,128]{3,2,1,0:T(4,128)(2,1)S(1)}, u32[]{:S(2)}, u32[]{:S(2)}) async-start(bf16[12,256,4,128]{3,2,1,0:T(4,128)(2,1)} %get-tuple-element.152), calls=%async_computation.3 | async-start | bytes 6291456 | tf_op jit(solution)/shard_map/all_to_all | solution.py:90
  102.2 764.2 %all-reduce.3.cloned.1.call-start = ((), (), s32[]{:S(2)}) async-start(), calls=%async_computation.8 | async-start | bytes 131072
  144.6 4.2 copy-start.1
  148.8 4.2 copy-start.4
  152.9 231.2 %copy-start.2 = (bf16[8,4,128]{2,1,0:T(4,128)(2,1)S(1)}, bf16[8,4,128]{2,1,0:T(4,128)(2,1)}, u32[]{:S(2)}) copy-start(bf16[8,4,128]{2,1,0:T(4,128)(2,1)} %param.15) | copy-start | bytes 24580
  696.3 494.5 %reduce-scatter.3.cloned.1.call-start = ((), (), s32[]{:S(2)}) async-start(), calls=%async_computation.7 | async-start | bytes 8519680 | tf_op jit(solution)/shard_map/reduce_scatter | solution.py:107
  706.7 0.7 copy-start.5
Sparse Core Ops, SparseCore 0:
  13.1 99.7 all-gather.1
  696.4 169.9 all-reduce.2
  868.9 321.8 reduce-scatter.2
where the time goes:
time: 1250 us
  waiting for transfers between devices  512 us (41%)
  blocking collectives  406 us (32%)
  other arithmetic  172 us (14%)
  matrix products  89.4 us (7%)
  local copies, waits for them, and re-layouts  50.7 us (4%)
  between operations  13.8 us (1%)
    reduce_scatter x1, waiting for transfers between devices, local(): lax.psum_scatter(local_weighted * factor[..., None], ('store', 'ctx'), sc...  324 us
    pmax x1, blocking collectives, local(): lax.pmax(local_peak.astype(jnp.bfloat16), ('store', 'ctx'))  292 us
    unnamed x4, waiting for transfers between devices  158 us
    add x8, other arithmetic, merge_terms(): weighted_old * factor_old[..., None] + weighted_new * factor_new[..., None]  92.8 us
    all_to_all x1, blocking collectives, local(): lax.all_to_all(sent_keys, 'store', split_axis=0, concat_axis=0, tiled=True)  50.6 us
    all_to_all x1, blocking collectives, local(): lax.all_to_all(mixed_group, 'head', split_axis=0, concat_axis=1, tiled=True)  49.5 us
    dot_general x9, matrix products, block_terms(): jnp.einsum('rgqk,kgd->rgqd', weights, value_tile, preferred_element_type=...  48.8 us
    reduce_sum x9, other arithmetic, block_terms(): total_sum = jnp.sum(weights.astype(jnp.float32), axis=3)  46.8 us
  transfers between devices with their start and end apart: 4, of which 3 were waited for; matrix products, arithmetic and copies ran while one was open for 5% of the time, Pallas kernels for 0%

commit v1 on v0

v1 whole, which is shorter than its diff:
```python
import functools
import math

import jax
import jax.numpy as jnp
from jax import lax
from jax.experimental import pallas as pl
from jax.experimental.pallas import tpu as pltpu
from jax.sharding import PartitionSpec as P

NEG = -1e30
EXP2_SCALE = math.log2(math.e) / math.sqrt(128)
NT = (((1,), (1,)), ((), ()))
NN = (((1,), (0,)), ((), ()))
MESH = pl.DeviceIdType.MESH
PARTS = ((0, 80), (80, 80), (160, 96))
JOBS = 12
TOP16 = 32767.0


def matmul(a, b, dims=NN):
    return lax.dot_general(a, b, dims, preferred_element_type=jnp.float32)


def position():
    ctx = lax.axis_index("ctx")
    return [lax.axis_index("store"), ctx // 4, ctx % 4], lax.axis_index("head")


def device(place, core):
    return (place[0], place[1] * 4 + place[2], core)


def along(place, axis, step):
    moved = list(place)
    moved[axis] = (place[axis] + step) % 4
    return moved


def greet(place, core):
    barrier = pltpu.get_barrier_semaphore()
    for axis in range(3):
        for step in (1, 2, 3):
            pl.semaphore_signal(barrier, 1, device_id=device(along(place, axis, step), core), device_id_type=MESH)
    pl.semaphore_signal(barrier, 1, device_id=device(place, 1 - core), device_id_type=MESH)
    pl.semaphore_wait(barrier, 10)


def gather_kernel(q_ref, list_ref, all_ref, lists_ref, mine, theirs, send, own, swap_sem, list_sem, own_sem, send_sem, recv_sem):
    place, core = position()
    greet(place, core)
    swap = pltpu.make_async_remote_copy(
        q_ref.at[:, pl.ds((1 - core) * 32, 32), :], theirs, swap_sem.at[0], swap_sem.at[1],
        device_id=device(place, 1 - core), device_id_type=MESH)
    swap.start()
    lists = []
    for step in (1, 2, 3):
        copy = pltpu.make_async_remote_copy(
            list_ref, lists_ref.at[place[0]], list_sem.at[0, step - 1], list_sem.at[1, step - 1],
            device_id=device(along(place, 0, step), core), device_id_type=MESH)
        copy.start()
        lists.append(copy)
    own_lists = pltpu.make_async_copy(list_ref, lists_ref.at[place[0]], own_sem.at[1])
    own_lists.start()

    def grouped(tokens):
        wide = tokens.astype(jnp.float32).reshape(4, 4, 8, 128)
        return jnp.stack([wide[:, g].reshape(32, 128) for g in range(4)]).astype(jnp.bfloat16)

    mine[...] = q_ref[:, pl.ds(core * 32, 32), :]
    send[:, pl.ds(core * 32, 32), :] = grouped(mine[...])
    swap.wait()
    send[:, pl.ds((1 - core) * 32, 32), :] = grouped(theirs[...])
    own[...] = send[...].reshape(256, 128)
    keep = pltpu.make_async_copy(own, all_ref.at[place[0], place[1], place[2]], own_sem.at[0])
    keep.start()

    def copies(part, phase):
        order = [(part + i) % 3 for i in range(3)]
        rows = pl.ds(*PARTS[part])
        where = [slice(None) if axis in order[:phase] else place[axis] for axis in range(3)]
        block = all_ref.at[where[0], where[1], where[2], rows]
        source = own.at[rows] if phase == 0 else block
        return [
            pltpu.make_async_remote_copy(
                source, block, send_sem.at[part, phase, step - 1], recv_sem.at[part, phase, step - 1],
                device_id=device(along(place, order[phase], step), core), device_id_type=MESH)
            for step in (1, 2, 3)
        ]

    started = []
    for phase in range(3):
        for part in range(3):
            if phase:
                for copy in started[(phase - 1) * 3 + part]:
                    copy.wait_recv()
            elif part == 0:
                pass
            if phase == 1 and part == 0:
                keep.wait()
            now = copies(part, phase)
            for copy in now:
                copy.start()
            started.append(now)
    for part in range(3):
        for copy in started[6 + part]:
            copy.wait_recv()
    for group in started:
        for copy in group:
            copy.wait_send()
    for copy in lists:
        copy.wait()
    own_lists.wait()


def gather_queries(queries, lists):
    hbm = pl.BlockSpec(memory_space=pl.ANY)
    vmem = pl.BlockSpec(memory_space=pltpu.VMEM)
    dma = pltpu.SemaphoreType.DMA
    return pl.pallas_call(
        gather_kernel,
        out_shape=[jax.ShapeDtypeStruct((4, 4, 4, 256, 128), jnp.bfloat16), jax.ShapeDtypeStruct((4, 8, 128), jnp.int32)],
        in_specs=[vmem, vmem],
        out_specs=[hbm, hbm],
        scratch_shapes=[
            pltpu.VMEM((4, 32, 128), jnp.bfloat16), pltpu.VMEM((4, 32, 128), jnp.bfloat16),
            pltpu.VMEM((4, 64, 128), jnp.bfloat16), pltpu.VMEM((256, 128), jnp.bfloat16),
            dma((2,)), dma((2, 3)), dma((2,)), dma((3, 3, 3)), dma((3, 3, 3)),
        ],
        compiler_params=pltpu.CompilerParams(collective_id=0, has_side_effects=True, vmem_limit_bytes=16 * 2**20),
        name="gather_queries",
    )(queries, lists)


def attend_kernel(list_ref, q_ref, pk_ref, pv_ref, sk_ref, sv_ref, o_ref, side_ref,
                  kj, vj, peak, acc, jobs, count, sem):
    @pl.when(pl.program_id(0) == 0)
    def prepare():
        store = lax.axis_index("store")
        count[0] = 0

        def look(i, _):
            row, e = i // 8, i % 8
            slot, valid = list_ref[row, 1, e], list_ref[row, 2, e]

            @pl.when((list_ref[row, 0, e] == store) & (valid > 0))
            def _():
                n = count[0]
                jobs[0, n] = slot
                jobs[1, n] = valid
                count[0] = n + 1
                pltpu.make_async_copy(pk_ref.at[slot], kj.at[n], sem.at[0, n]).start()
                pltpu.make_async_copy(pv_ref.at[slot], vj.at[n, :, 0:128], sem.at[1, n]).start()
            return 0

        lax.fori_loop(0, 32, look, 0)

        def fix(n, _):
            slot, valid = jobs[0, n], jobs[1, n]
            pltpu.make_async_copy(pk_ref.at[slot], kj.at[n], sem.at[0, n]).wait()
            pltpu.make_async_copy(pv_ref.at[slot], vj.at[n, :, 0:128], sem.at[1, n]).wait()
            live_row = lax.broadcasted_iota(jnp.int32, (256, 128), 0) < valid
            live_lane = lax.broadcasted_iota(jnp.int32, (128, 256), 1) < valid
            for g in range(4):
                keys = kj[n, g].astype(jnp.float32)
                kj[n, g] = jnp.where(live_row, keys, keys[0:1]).astype(jnp.bfloat16)
                vj[n, g, 0:128] = jnp.where(live_lane, vj[n, g, 0:128].astype(jnp.float32), 0.0).astype(jnp.bfloat16)
                vj[n, g, 128:144] = live_lane[0:16].astype(jnp.float32).astype(jnp.bfloat16)
            return 0

        lax.fori_loop(0, count[0], fix, 0)

    pair = pl.program_id(0)
    suffix_at = (lax.axis_index("store") * 16 + lax.axis_index("ctx")) * 8
    key_at = suffix_at + lax.broadcasted_iota(jnp.int32, (8, 4096), 0)
    query_at = lax.broadcasted_iota(jnp.int32, (8, 4096), 1) // 8
    live = key_at <= query_at
    for half in range(2):
        q = q_ref[:, half * 64:(half + 1) * 64, :].reshape(4096, 128)
        s = matmul(sk_ref[pair * 2 + half], q, NT)[0:8]
        s = jnp.where(live, s, NEG)
        t = jnp.max(s, axis=0, keepdims=True)
        w = jnp.where(live, jnp.exp2((s - t) * EXP2_SCALE), 0.0)
        w = jnp.concatenate([w, jnp.zeros((120, 4096), jnp.float32)], axis=0).astype(jnp.bfloat16)
        acc[half] = matmul(sv_ref[pair * 2 + half], w)
        peak[half] = t

        def block(n, _):
            s = matmul(kj[n, pair * 2 + half], q, NT)
            t = jnp.max(s, axis=0, keepdims=True)
            w = jnp.exp2((s - t) * EXP2_SCALE).astype(jnp.bfloat16)
            x = matmul(vj[n, pair * 2 + half], w)
            m = peak[half]
            top = jnp.maximum(m, t)
            acc[half] = acc[half] * jnp.exp2((m - top) * EXP2_SCALE) + x * jnp.exp2((t - top) * EXP2_SCALE)
            peak[half] = top
            return 0

        lax.fori_loop(0, count[0], block, 0)

    low = lax.broadcasted_iota(jnp.int32, (1, 128), 1) < 64

    def emit(i, _):
        lanes = pl.ds(pl.multiple_of(i * 128, 128), 128)
        a, b = acc[0, 0:136, lanes], acc[1, 0:136, lanes]
        pa, pb = peak[0, :, lanes], peak[1, :, lanes]
        for odd in range(2):
            if odd:
                whole = jnp.where(low, pltpu.roll(a, 64, 1), b)
                top = jnp.where(low, pltpu.roll(jnp.broadcast_to(pa, (8, 128)), 64, 1)[0:1], pb)
            else:
                whole = jnp.where(low, a, pltpu.roll(b, 64, 1))
                top = jnp.where(low, pa, pltpu.roll(jnp.broadcast_to(pb, (8, 128)), 64, 1)[0:1])
            values, scale = encode(whole[0:128])
            o_ref[i * 2 + odd, 0] = values
            side_ref[i * 2 + odd, 0] = jnp.concatenate([top, whole[128:129], scale, jnp.zeros((5, 128), jnp.float32)], axis=0)
        return 0

    lax.fori_loop(0, 32, emit, 0)


def encode(x):
    largest = jnp.maximum(jnp.max(jnp.abs(x), axis=0, keepdims=True), 1e-30)
    whole = jnp.round(x * (TOP16 / largest)).astype(jnp.int32).astype(jnp.int16)
    return whole, largest * (1.0 / TOP16)


def attend(lists, gathered, pool_k, pool_v, suffix_k, suffix_v):
    hbm = pl.BlockSpec(memory_space=pl.ANY)
    return pl.pallas_call(
        attend_kernel,
        grid=(2,),
        in_specs=[
            pl.BlockSpec(memory_space=pltpu.SMEM),
            pl.BlockSpec((64, 128, 128), lambda i: (0, i, 0)),
            hbm, hbm,
            pl.BlockSpec((4, 16, 128), lambda i: (0, 0, 0)),
            pl.BlockSpec((4, 144, 128), lambda i: (0, 0, 0)),
        ],
        out_specs=[pl.BlockSpec((64, 1, 128, 128), lambda i: (0, i, 0, 0)), pl.BlockSpec((64, 1, 8, 128), lambda i: (0, i, 0, 0))],
        out_shape=[jax.ShapeDtypeStruct((64, 2, 128, 128), jnp.int16), jax.ShapeDtypeStruct((64, 2, 8, 128), jnp.float32)],
        scratch_shapes=[
            pltpu.VMEM((JOBS, 4, 256, 128), jnp.bfloat16), pltpu.VMEM((JOBS, 4, 144, 256), jnp.bfloat16),
            pltpu.VMEM((2, 1, 4096), jnp.float32), pltpu.VMEM((2, 144, 4096), jnp.float32),
            pltpu.SMEM((2, JOBS), jnp.int32), pltpu.SMEM((1,), jnp.int32), pltpu.SemaphoreType.DMA((2, JOBS)),
        ],
        compiler_params=pltpu.CompilerParams(vmem_limit_bytes=60 * 2**20),
        name="attend",
    )(lists, gathered, pool_k, pool_v, suffix_k, suffix_v)


def merge(parts):
    top = functools.reduce(jnp.maximum, [side[0:1] for _, side in parts])
    total, weighted = 0.0, 0.0
    for values, side in parts:
        factor = jnp.exp2((side[0:1] - top) * EXP2_SCALE)
        total = total + side[1:2] * factor
        weighted = weighted + values.astype(jnp.int32).astype(jnp.float32) * (side[2:3] * factor)
    return weighted, top, total


def merge_kernel(o_ref, side_ref, out_ref, r1, r1s, p1, p1s, r2, r2s, p2, p2s, r3, r3s, rows, swapped, wide,
                 send1, recv1, send2, recv2, send3, recv3, swap_sem):
    place, core = position()
    greet(place, core)

    def least(color, a, u):
        return (color - a - u + 9) % 3

    def number(color, a, u, v):
        at = [None] * 3
        for axis, value in zip([(color + i) % 3 for i in range(3)], (a, u, v)):
            at[axis] = value
        return at[0] * 16 + at[1] * 4 + at[2]

    def two(source, source_side, target, target_side, send, recv, to):
        return [
            pltpu.make_async_remote_copy(source, target, send.at[0], recv.at[0], device_id=to, device_id_type=MESH),
            pltpu.make_async_remote_copy(source_side, target_side, send.at[1], recv.at[1], device_id=to, device_id_type=MESH),
        ]

    def first(color, step, w):
        a = (place[color] + step) % 4
        u = w // 2
        v = least(color, a, u) + 3 * (w % 2)
        chunk = jnp.minimum(number(color, a, u, v), 63)
        return v <= 3, two(
            o_ref.at[chunk], side_ref.at[chunk], r1.at[color, step - 1, w], r1s.at[color, step - 1, w],
            send1.at[color, step - 1, w], recv1.at[color, step - 1, w], device(along(place, color, step), core))

    def each(function):
        for color in range(3):
            for step in (2, 1, 3):
                def go(w, _):
                    there, copies = first(color, step, w)

                    @pl.when(there)
                    def _():
                        for copy in copies:
                            function(copy)
                    return 0
                lax.fori_loop(0, 8, go, 0)

    each(lambda copy: copy.start())

    def second(color, u, half):
        axis = (color + 1) % 3
        step = (u - place[axis] + 4) % 4
        to = list(place)
        to[axis] = u
        at = jnp.maximum(step - 1, 0)
        return two(p1.at[color, u * 2 + half], p1s.at[color, u * 2 + half], r2.at[color, at, half], r2s.at[color, at, half],
                   send2.at[color, at, half], recv2.at[color, at, half], device(to, core))

    def fold(sources, target, target_side):
        for pair in range(2):
            weighted, top, total = merge([(values[pair], side[pair]) for values, side in sources])
            values, scale = encode(weighted)
            target[pair] = values
            target_side[pair] = jnp.concatenate([top, total, scale, jnp.zeros((5, 128), jnp.float32)], axis=0)

    for color in range(3):
        a = place[color]
        second_at = place[(color + 1) % 3]

        def go(w, _):
            u = w // 2
            v = least(color, a, u) + 3 * (w % 2)

            @pl.when(v <= 3)
            def _():
                for step in (1, 2, 3):
                    for copy in first(color, step, w)[1]:
                        copy.wait_recv()
                chunk = jnp.minimum(number(color, a, u, v), 63)
                fold([(o_ref.at[chunk], side_ref.at[chunk])]
                     + [(r1.at[color, k, w], r1s.at[color, k, w]) for k in range(3)],
                     p1.at[color, w], p1s.at[color, w])

                @pl.when(u != second_at)
                def _():
                    for copy in second(color, u, w % 2):
                        copy.start()
            return 0

        lax.fori_loop(0, 8, go, 0)

    def third(color, half, v):
        axis = (color + 2) % 3
        at = jnp.maximum((v - place[axis] + 4) % 4 - 1, 0)
        to = list(place)
        to[axis] = v
        return two(p2.at[color, half], p2s.at[color, half], r3.at[at], r3s.at[at],
                   send3.at[color, at], recv3.at[at], device(to, core))

    for color in range(3):
        a, b, c = place[color], place[(color + 1) % 3], place[(color + 2) % 3]
        for half in range(2):
            v = least(color, a, b) + 3 * half

            @pl.when(v <= 3)
            def _():
                for k in range(3):
                    for copy in two(p1.at[color, 0], p1s.at[color, 0], r2.at[color, k, half], r2s.at[color, k, half],
                                    send2.at[color, k, half], recv2.at[color, k, half], device(along(place, (color + 1) % 3, 1), core)):
                        copy.wait_recv()
                slot = b * 2 + half
                fold([(p1.at[color, slot], p1s.at[color, slot])]
                     + [(r2.at[color, k, half], r2s.at[color, k, half]) for k in range(3)],
                     p2.at[color, half], p2s.at[color, half])

                @pl.when(v != c)
                def _():
                    for copy in third(color, half, v):
                        copy.start()

    color = (place[0] + place[1] + place[2]) % 3
    for k in range(3):
        for copy in two(p2.at[0, 0], p2s.at[0, 0], r3.at[k], r3s.at[k], send3.at[0, k], recv3.at[k],
                        device(along(place, 0, 1), core)):
            copy.wait_recv()
    third_at = jnp.where(color == 0, place[2], jnp.where(color == 1, place[0], place[1]))
    half = third_at // 3
    mine = [(p2.at[color, half], p2s.at[color, half])] + [(r3.at[k], r3s.at[k]) for k in range(3)]
    for pair in range(2):
        weighted, top, total = merge([(values[pair], side[pair]) for values, side in mine])
        done = jnp.transpose(weighted / total)
        for g in range(2):
            for owner in range(2):
                rows[owner, pair * 2 + g] = done[g * 64 + owner * 32:g * 64 + (owner + 1) * 32]
    swap = pltpu.make_async_remote_copy(rows.at[1 - core], swapped, swap_sem.at[0], swap_sem.at[1],
                                        device_id=device(place, 1 - core), device_id_type=MESH)
    swap.start()

    def tokens(grouped):
        split = grouped.reshape(4, 4, 8, 128)
        return jnp.stack([jnp.concatenate([split[g, t] for g in range(4)], axis=0) for t in range(4)])

    wide[:, pl.ds(pl.multiple_of(core * 32, 32), 32), :] = tokens(rows[core])
    swap.wait()
    wide[:, pl.ds(pl.multiple_of((1 - core) * 32, 32), 32), :] = tokens(swapped[...])
    out_ref[...] = wide[...].astype(jnp.bfloat16)

    each(lambda copy: copy.wait_send())
    for color in range(3):
        a, b, c = place[color], place[(color + 1) % 3], place[(color + 2) % 3]

        def go(w, _):
            u = w // 2

            @pl.when((least(color, a, u) + 3 * (w % 2) <= 3) & (u != b))
            def _():
                for copy in second(color, u, w % 2):
                    copy.wait_send()
            return 0

        lax.fori_loop(0, 8, go, 0)
        for half in range(2):
            v = least(color, a, b) + 3 * half

            @pl.when((v <= 3) & (v != c))
            def _():
                for copy in third(color, half, v):
                    copy.wait_send()


def merge_parts(values, side):
    vmem = pl.BlockSpec(memory_space=pltpu.VMEM)
    dma = pltpu.SemaphoreType.DMA

    def both(*lead):
        return [pltpu.VMEM((*lead, 2, 128, 128), jnp.int16), pltpu.VMEM((*lead, 2, 8, 128), jnp.float32)]

    return pl.pallas_call(
        merge_kernel,
        out_shape=jax.ShapeDtypeStruct((4, 64, 128), jnp.bfloat16),
        in_specs=[vmem, vmem],
        out_specs=vmem,
        scratch_shapes=[
            *both(3, 3, 8), *both(3, 8), *both(3, 3, 2), *both(3, 2), *both(3),
            pltpu.VMEM((2, 4, 32, 128), jnp.float32), pltpu.VMEM((4, 32, 128), jnp.float32), pltpu.VMEM((4, 64, 128), jnp.float32),
            dma((3, 3, 8, 2)), dma((3, 3, 8, 2)), dma((3, 3, 2, 2)), dma((3, 3, 2, 2)), dma((3, 3, 2)), dma((3, 2)), dma((2,)),
        ],
        compiler_params=pltpu.CompilerParams(collective_id=1, has_side_effects=True, vmem_limit_bytes=48 * 2**20),
        name="merge_parts",
    )(values, side)


def local(queries, suffix_k, suffix_v, pool_k, pool_v, list_holder, list_slot, list_valid):
    lists = jnp.zeros((8, 128), jnp.int32).at[0:3, 0:8].set(jnp.stack([list_holder[:, 0], list_slot, list_valid]))
    gathered, every_list = gather_queries(queries, lists)
    keys = jnp.transpose(pool_k, (0, 2, 1, 3))
    values = jnp.transpose(pool_v, (0, 2, 3, 1))
    near_k = jnp.pad(jnp.transpose(suffix_k, (1, 0, 2)), ((0, 0), (0, 8), (0, 0)))
    near_v = jnp.concatenate([jnp.transpose(suffix_v, (1, 2, 0)), jnp.ones((4, 16, 8), jnp.bfloat16)], axis=1)
    near_v = jnp.pad(near_v, ((0, 0), (0, 0), (0, 120)))
    parts, side = attend(every_list, gathered.reshape(64, 256, 128), keys, values, near_k, near_v)
    return merge_parts(parts, side)


def solution(mesh):
    in_specs = (
        P(("store", "ctx", "head"), None, None),
        P(("store", "ctx"), "head", None),
        P(("store", "ctx"), "head", None),
        P(("store", "ctx"), None, "head", None),
        P(("store", "ctx"), None, "head", None),
        P(("store", "ctx"), None),
        P(("store", "ctx")),
        P(("store", "ctx")),
    )
    out_specs = P(("store", "ctx", "head"), None, None)
    return jax.shard_map(local, mesh=mesh, in_specs=in_specs, out_specs=out_specs, check_vma=False)
```

time: 1250 us -> 191 us (0.15)
  the two profiles are of different devices: /device:TPU:1 before, /device:TPU:5 now
where the time goes in v1:
time: 191 us
  Pallas kernels  168 us (88%)
  local copies, waits for them, and re-layouts  21.2 us (11%)
    pallas_call x1, Pallas kernels, merge_parts(): pl.pallas_call(merge_kernel, out_shape=jax.ShapeDtypeStruct((4, 64, 128),...  72.2 us
    pallas_call x1, Pallas kernels, attend(): pl.pallas_call(attend_kernel, grid=(2,), in_specs=[pl.BlockSpec(memory_sp...  61.1 us
    pallas_call x1, Pallas kernels, gather_queries(): pl.pallas_call(gather_kernel, out_shape=[jax.ShapeDtypeStruct((4, 4, 4, 2...  34.8 us
    unnamed x15, local copies, waits for them, and re-layouts  20.6 us

profile of v1, /device:TPU:5, one launch (start us, length us, event | category | flops | bytes accessed | tf_op | source)
XLA Modules:
  0.0 190.7 jit_solution(9011947335718444316)
XLA Ops:
  0.0 0.7 pad_add_fusion
  0.7 0.7 copy.16
  1.4 0.6 pad.15.sk_ref
  2.0 0.9 copy.12
  2.9 0.7 fusion.sv_ref
  3.6 5.3 %copy.15 = bf16[16,256,4,128]{3,1,2,0:T(8,128)(2,1)} copy(bf16[16,256,4,128]{3,2,1,0:T(4,128)(2,1)} %param.13) | data formatting | bytes 8388608 | tf_op args[3]
  8.9 0.0 copy-start.3
  8.9 7.4 %copy.10 = bf16[16,256,4,128]{1,3,2,0:T(8,128)(2,1)} copy(bf16[16,256,4,128]{3,2,1,0:T(4,128)(2,1)} %param.14) | data formatting | bytes 8388608 | tf_op args[4]
  16.2 0.0 copy-done.3
  16.2 34.8 %gather_queries.1 = (bf16[4,4,4,256,128]{4,3,2,1,0:T(8,128)(2,1)S(1)}, s32[4,8,128]{2,1,0:T(8,128)S(1)}) custom-call(bf16[4,64,128]{2,1,0:T(8,128)(2,1)S(1)} %copy-done.3, s32[8,128]{1,0:T(8,128)S(1)} %scatter.4.list_ref), custom_call_target="tpu_custom_call" | custom-call | tf_op jit(solution)/shard_map/gather_queries/pallas_call | solution.py:120
  51.0 0.0 copy-start.1
  51.0 1.9 %copy-done.1 = bf16[4,4,4,256,128]{4,3,2,1,0:T(8,128)(2,1)} copy-done((bf16[4,4,4,256,128]{4,3,2,1,0:T(8,128)(2,1)}, bf16[4,4,4,256,128]{4,3,2,1,0:T(8,128)(2,1)S(1)}, u32[]{:S(2)}) %copy-start.1) | copy-done | bytes 4194328
  52.9 0.0 copy-start.4
  52.9 0.6 copy-done.4
  53.5 61.1 %attend.1 = (s16[64,2,128,128]{3,2,1,0:T(8,128)(2,1)}, f32[64,2,8,128]{3,2,1,0:T(8,128)}) custom-call(s32[4,8,128]{2,1,0:T(8,128)} %copy-done.4, bf16[64,256,128]{2,1,0:T(8,128)(2,1)} %bitcast.12, bf16[16,4,256,128]{3,2,1,0:T(8,128)(2,1)} %bitcast.13, bf16[16,4,128,256]{3,2,1,0:T(8,128)(2,1)} %bitcast.14, bf16[4,16,128]{2,1,0:T(8,128)(2,1)} %pad.15.sk_ref, ...), custom_call_target="tpu_custom_call" | custom-call | tf_op jit(solution)/shard_map/attend/pallas_call | solution.py:230
  114.7 0.0 copy-start
  114.7 2.2 %copy-done = s16[64,2,128,128]{3,2,1,0:T(8,128)(2,1)S(1)} copy-done((s16[64,2,128,128]{3,2,1,0:T(8,128)(2,1)S(1)}, s16[64,2,128,128]{3,2,1,0:T(8,128)(2,1)}, u32[]{:S(2)}) %copy-start) | copy-done | bytes 4194328
  116.9 0.0 copy-start.2
  116.9 1.0 copy-done.2
  117.9 72.2 %merge_parts.1 = bf16[4,64,128]{2,1,0:T(8,128)(2,1)S(1)} custom-call(s16[64,2,128,128]{3,2,1,0:T(8,128)(2,1)S(1)} %copy-done, f32[64,2,8,128]{3,2,1,0:T(8,128)S(1)} %copy-done.2), custom_call_target="tpu_custom_call" | custom-call | tf_op jit(solution)/shard_map/merge_parts/pallas_call | solution.py:434
  190.1 0.6 copy.18
  (1 shorter events, 0.0 us)
Async XLA Ops:
  8.9 7.4 %copy-start.3 = (bf16[4,64,128]{2,1,0:T(8,128)(2,1)S(1)}, bf16[4,64,128]{2,1,0:T(8,128)(2,1)}, u32[]{:S(2)}) copy-start(bf16[4,64,128]{2,1,0:T(8,128)(2,1)} %q_ref.1) | copy-start | bytes 196612
  51.0 1.9 %copy-start.1 = (bf16[4,4,4,256,128]{4,3,2,1,0:T(8,128)(2,1)}, bf16[4,4,4,256,128]{4,3,2,1,0:T(8,128)(2,1)S(1)}, u32[]{:S(2)}) copy-start(bf16[4,4,4,256,128]{4,3,2,1,0:T(8,128)(2,1)S(1)} %get-tuple-element.22) | copy-start | bytes 12582916
  52.9 0.6 copy-start.4
  114.7 2.2 %copy-start = (s16[64,2,128,128]{3,2,1,0:T(8,128)(2,1)S(1)}, s16[64,2,128,128]{3,2,1,0:T(8,128)(2,1)}, u32[]{:S(2)}) copy-start(s16[64,2,128,128]{3,2,1,0:T(8,128)(2,1)} %get-tuple-element.23.o_ref) | copy-start | bytes 12582916
  116.9 1.0 copy-start.2

commit v2 on v1

--- a/solution.py
+++ b/solution.py
@@ -46,8 +46,37 @@
     pl.semaphore_wait(barrier, 10)
 
 
-def gather_kernel(q_ref, list_ref, all_ref, lists_ref, mine, theirs, send, own, swap_sem, list_sem, own_sem, send_sem, recv_sem):
+def gather_kernel(q_ref, holder_ref, slot_ref, valid_ref, pk_ref, pv_ref, all_ref, lists_ref, kp_ref, vp_ref,
+                  list_ref, theirs, send, own, raw_k, raw_v, keys, values, wide_k, wide_v,
+                  swap_sem, list_sem, own_sem, send_sem, recv_sem, raw_sem, out_sem):
     place, core = position()
+
+    def raw_copies(n):
+        return [pltpu.make_async_copy(pk_ref.at[n], raw_k.at[n], raw_sem.at[0, n]),
+                pltpu.make_async_copy(pv_ref.at[n], raw_v.at[n], raw_sem.at[1, n])]
+
+    def out_copies(n):
+        return [pltpu.make_async_copy(keys.at[n], kp_ref.at[n], out_sem.at[0, n]),
+                pltpu.make_async_copy(values.at[n], vp_ref.at[n], out_sem.at[1, n])]
+
+    def over(first, last, function):
+        def go(n, _):
+            function(n)
+            return 0
+        lax.fori_loop(first, last, go, 0)
+
+    def begin(n):
+        for copy in raw_copies(n):
+            copy.start()
+
+    over(0, 16, begin)
+    row = lax.broadcasted_iota(jnp.int32, (8, 128), 0)
+    lane = lax.broadcasted_iota(jnp.int32, (8, 128), 1)
+    tile = jnp.zeros((8, 128), jnp.int32)
+    for e in range(8):
+        for r, ref in enumerate((holder_ref, slot_ref, valid_ref)):
+            tile = jnp.where((row == r) & (lane == e), ref[e], tile)
+    list_ref[...] = tile
     greet(place, core)
     swap = pltpu.make_async_remote_copy(
         q_ref.at[:, pl.ds((1 - core) * 32, 32), :], theirs, swap_sem.at[0], swap_sem.at[1],
@@ -67,8 +96,18 @@
         wide = tokens.astype(jnp.float32).reshape(4, 4, 8, 128)
         return jnp.stack([wide[:, g].reshape(32, 128) for g in range(4)]).astype(jnp.bfloat16)
 
-    mine[...] = q_ref[:, pl.ds(core * 32, 32), :]
-    send[:, pl.ds(core * 32, 32), :] = grouped(mine[...])
+    def regroup(n):
+        for copy in raw_copies(n):
+            copy.wait()
+        wide_k[...] = raw_k[n].astype(jnp.float32)
+        wide_v[...] = raw_v[n].astype(jnp.float32)
+        for g in range(4):
+            keys[n, g] = wide_k[pl.ds(g, 256, stride=4), :].astype(jnp.bfloat16)
+            values[n, g] = jnp.transpose(wide_v[pl.ds(g, 256, stride=4), :]).astype(jnp.bfloat16)
+        for copy in out_copies(n):
+            copy.start()
+
+    send[:, pl.ds(core * 32, 32), :] = grouped(q_ref[:, pl.ds(core * 32, 32), :])
     swap.wait()
     send[:, pl.ds((1 - core) * 32, 32), :] = grouped(theirs[...])
     own[...] = send[...].reshape(256, 128)
@@ -94,14 +133,13 @@
             if phase:
                 for copy in started[(phase - 1) * 3 + part]:
                     copy.wait_recv()
-            elif part == 0:
-                pass
             if phase == 1 and part == 0:
                 keep.wait()
             now = copies(part, phase)
             for copy in now:
                 copy.start()
             started.append(now)
+        over(*((0, 3), (3, 7), (7, 16))[phase], regroup)
     for part in range(3):
         for copy in started[6 + part]:
             copy.wait_recv()
@@ -112,32 +150,45 @@
         copy.wait()
     own_lists.wait()
 
-
-def gather_queries(queries, lists):
+    def finish(n):
+        for copy in out_copies(n):
+            copy.wait()
+
+    over(0, 16, finish)
+
+
+def gather_queries(queries, holder, slot, valid, pool_k, pool_v):
     hbm = pl.BlockSpec(memory_space=pl.ANY)
-    vmem = pl.BlockSpec(memory_space=pltpu.VMEM)
+    vmem, smem = pl.BlockSpec(memory_space=pltpu.VMEM), pl.BlockSpec(memory_space=pltpu.SMEM)
     dma = pltpu.SemaphoreType.DMA
     return pl.pallas_call(
         gather_kernel,
-        out_shape=[jax.ShapeDtypeStruct((4, 4, 4, 256, 128), jnp.bfloat16), jax.ShapeDtypeStruct((4, 8, 128), jnp.int32)],
-        in_specs=[vmem, vmem],
-        out_specs=[hbm, hbm],
+        out_shape=[
+            jax.ShapeDtypeStruct((4, 4, 4, 256, 128), jnp.bfloat16), jax.ShapeDtypeStruct((4, 8, 128), jnp.int32),
+            jax.ShapeDtypeStruct((16, 4, 256, 128), jnp.bfloat16), jax.ShapeDtypeStruct((16, 4, 128, 256), jnp.bfloat16),
+        ],
+        in_specs=[vmem, smem, smem, smem, hbm, hbm],
+        out_specs=[hbm] * 4,
         scratch_shapes=[
-            pltpu.VMEM((4, 32, 128), jnp.bfloat16), pltpu.VMEM((4, 32, 128), jnp.bfloat16),
+            pltpu.VMEM((8, 128), jnp.int32), pltpu.VMEM((4, 32, 128), jnp.bfloat16),
             pltpu.VMEM((4, 64, 128), jnp.bfloat16), pltpu.VMEM((256, 128), jnp.bfloat16),
-            dma((2,)), dma((2, 3)), dma((2,)), dma((3, 3, 3)), dma((3, 3, 3)),
+            pltpu.VMEM((16, 1024, 128), jnp.bfloat16), pltpu.VMEM((16, 1024, 128), jnp.bfloat16),
+            pltpu.VMEM((16, 4, 256, 128), jnp.bfloat16), pltpu.VMEM((16, 4, 128, 256), jnp.bfloat16),
+            pltpu.VMEM((1024, 128), jnp.float32), pltpu.VMEM((1024, 128), jnp.float32),
+            dma((2,)), dma((2, 3)), dma((2,)), dma((3, 3, 3)), dma((3, 3, 3)), dma((2, 16)), dma((2, 16)),
         ],
-        compiler_params=pltpu.CompilerParams(collective_id=0, has_side_effects=True, vmem_limit_bytes=16 * 2**20),
+        compiler_params=pltpu.CompilerParams(collective_id=0, has_side_effects=True, vmem_limit_bytes=62 * 2**20),
         name="gather_queries",
-    )(queries, lists)
-
-
-def attend_kernel(list_ref, q_ref, pk_ref, pv_ref, sk_ref, sv_ref, o_ref, side_ref,
-                  kj, vj, peak, acc, jobs, count, sem):
+    )(queries, holder, slot, valid, pool_k, pool_v)
+
+
+def attend_kernel(list_ref, q_ref, pk_ref, pv_ref, near_k_ref, near_v_ref, o_ref, side_ref,
+                  kj, vj, sk_ref, sv_ref, near, peak, acc, jobs, count, sem):
     @pl.when(pl.program_id(0) == 0)
     def prepare():
         store = lax.axis_index("store")
         count[0] = 0
+        count[1] = 0
 
         def look(i, _):
             row, e = i // 8, i % 8
@@ -145,15 +196,25 @@
 
             @pl.when((list_ref[row, 0, e] == store) & (valid > 0))
             def _():
-                n = count[0]
+                long = valid > 128
+                n = jnp.where(long, count[0], JOBS - 1 - count[1])
                 jobs[0, n] = slot
                 jobs[1, n] = valid
-                count[0] = n + 1
+                count[0] = count[0] + jnp.where(long, 1, 0)
+                count[1] = count[1] + jnp.where(long, 0, 1)
                 pltpu.make_async_copy(pk_ref.at[slot], kj.at[n], sem.at[0, n]).start()
                 pltpu.make_async_copy(pv_ref.at[slot], vj.at[n, :, 0:128], sem.at[1, n]).start()
             return 0
 
         lax.fori_loop(0, 32, look, 0)
+        near[0] = near_k_ref[...].astype(jnp.float32)
+        near[1] = near_v_ref[...].astype(jnp.float32)
+        ones = jnp.where(lax.broadcasted_iota(jnp.int32, (16, 128), 1) < 8, 1.0, 0.0)
+        for g in range(4):
+            k, v = near[0, pl.ds(g, 8, stride=4), :], near[1, pl.ds(g, 8, stride=4), :]
+            sk_ref[g] = jnp.concatenate([k, jnp.zeros((8, 128), jnp.float32)], axis=0).astype(jnp.bfloat16)
+            v = jnp.transpose(jnp.concatenate([v, jnp.zeros((120, 128), jnp.float32)], axis=0))
+            sv_ref[g] = jnp.concatenate([v, ones], axis=0).astype(jnp.bfloat16)
 
         def fix(n, _):
             slot, valid = jobs[0, n], jobs[1, n]
@@ -169,6 +230,7 @@
             return 0
 
         lax.fori_loop(0, count[0], fix, 0)
+        lax.fori_loop(JOBS - count[1], JOBS, fix, 0)
 
     pair = pl.program_id(0)
     suffix_at = (lax.axis_index("store") * 16 + lax.axis_index("ctx")) * 8
@@ -185,18 +247,36 @@
         acc[half] = matmul(sv_ref[pair * 2 + half], w)
         peak[half] = t
 
-        def block(n, _):
-            s = matmul(kj[n, pair * 2 + half], q, NT)
-            t = jnp.max(s, axis=0, keepdims=True)
-            w = jnp.exp2((s - t) * EXP2_SCALE).astype(jnp.bfloat16)
-            x = matmul(vj[n, pair * 2 + half], w)
+        def unit(first, number, keys):
+            stack = kj[pl.ds(first, number), pair * 2 + half, 0:keys, :].reshape(number * keys, 128)
+            s = matmul(stack, q, NT)
             m = peak[half]
-            top = jnp.maximum(m, t)
-            acc[half] = acc[half] * jnp.exp2((m - top) * EXP2_SCALE) + x * jnp.exp2((t - top) * EXP2_SCALE)
+            tops, terms = [], []
+            for i in range(number):
+                part = s[i * keys:(i + 1) * keys]
+                t = jnp.max(part, axis=0, keepdims=True)
+                w = jnp.exp2((part - t) * EXP2_SCALE).astype(jnp.bfloat16)
+                terms.append(matmul(vj[first + i, pair * 2 + half, :, 0:keys], w))
+                tops.append(t)
+            top = functools.reduce(jnp.maximum, tops, m)
+            new = acc[half] * jnp.exp2((m - top) * EXP2_SCALE)
+            for t, x in zip(tops, terms):
+                new = new + x * jnp.exp2((t - top) * EXP2_SCALE)
+            acc[half] = new
             peak[half] = top
-            return 0
-
-        lax.fori_loop(0, count[0], block, 0)
+
+        def units(first, many, number, keys):
+            def go(i, _):
+                unit(first + i * number, number, keys)
+                return 0
+
+            lax.fori_loop(0, many, go, 0)
+
+        long, short = count[0], count[1]
+        units(0, long // 2, 2, 256)
+        units(long - long % 2, long % 2, 1, 256)
+        units(JOBS - short, short // 2, 2, 128)
+        units(JOBS - 1, short % 2, 1, 128)
 
     low = lax.broadcasted_iota(jnp.int32, (1, 128), 1) < 64
 
@@ -213,7 +293,7 @@
                 top = jnp.where(low, pa, pltpu.roll(jnp.broadcast_to(pb, (8, 128)), 64, 1)[0:1])
             values, scale = encode(whole[0:128])
             o_ref[i * 2 + odd, 0] = values
-            side_ref[i * 2 + odd, 0] = jnp.concatenate([top, whole[128:129], scale, jnp.zeros((5, 128), jnp.float32)], axis=0)
+            side_ref[i * 2 + odd, pl.ds(pair * 4, 4), :] = jnp.concatenate([top, whole[128:129], scale, scale], axis=0)
         return 0
 
     lax.fori_loop(0, 32, emit, 0)
@@ -234,17 +314,18 @@
             pl.BlockSpec(memory_space=pltpu.SMEM),
             pl.BlockSpec((64, 128, 128), lambda i: (0, i, 0)),
             hbm, hbm,
-            pl.BlockSpec((4, 16, 128), lambda i: (0, 0, 0)),
-            pl.BlockSpec((4, 144, 128), lambda i: (0, 0, 0)),
+            pl.BlockSpec((32, 128), lambda i: (0, 0)),
+            pl.BlockSpec((32, 128), lambda i: (0, 0)),
         ],
-        out_specs=[pl.BlockSpec((64, 1, 128, 128), lambda i: (0, i, 0, 0)), pl.BlockSpec((64, 1, 8, 128), lambda i: (0, i, 0, 0))],
-        out_shape=[jax.ShapeDtypeStruct((64, 2, 128, 128), jnp.int16), jax.ShapeDtypeStruct((64, 2, 8, 128), jnp.float32)],
+        out_specs=[pl.BlockSpec((64, 1, 128, 128), lambda i: (0, i, 0, 0)), pl.BlockSpec((64, 8, 128), lambda i: (0, 0, 0))],
+        out_shape=[jax.ShapeDtypeStruct((64, 2, 128, 128), jnp.int16), jax.ShapeDtypeStruct((64, 8, 128), jnp.float32)],
         scratch_shapes=[
             pltpu.VMEM((JOBS, 4, 256, 128), jnp.bfloat16), pltpu.VMEM((JOBS, 4, 144, 256), jnp.bfloat16),
+            pltpu.VMEM((4, 16, 128), jnp.bfloat16), pltpu.VMEM((4, 144, 128), jnp.bfloat16), pltpu.VMEM((2, 32, 128), jnp.float32),
             pltpu.VMEM((2, 1, 4096), jnp.float32), pltpu.VMEM((2, 144, 4096), jnp.float32),
-            pltpu.SMEM((2, JOBS), jnp.int32), pltpu.SMEM((1,), jnp.int32), pltpu.SemaphoreType.DMA((2, JOBS)),
+            pltpu.SMEM((2, JOBS), jnp.int32), pltpu.SMEM((2,), jnp.int32), pltpu.SemaphoreType.DMA((2, JOBS)),
         ],
-        compiler_params=pltpu.CompilerParams(vmem_limit_bytes=60 * 2**20),
+        compiler_params=pltpu.CompilerParams(vmem_limit_bytes=62 * 2**20),
         name="attend",
     )(lists, gathered, pool_k, pool_v, suffix_k, suffix_v)
 
@@ -259,10 +340,9 @@
     return weighted, top, total
 
 
-def merge_kernel(o_ref, side_ref, out_ref, r1, r1s, p1, p1s, r2, r2s, p2, p2s, r3, r3s, rows, swapped, wide,
-                 send1, recv1, send2, recv2, send3, recv3, swap_sem):
+def merge_kernel(o_ref, side_ref, out_ref, p0, p0s, r1, r1s, p1, p1s, r2, r2s, p2, p2s, r3, r3s, rows, swapped, wide,
+                 send1, recv1, send2, recv2, send3, recv3, swap_sem, own_sem):
     place, core = position()
-    greet(place, core)
 
     def least(color, a, u):
         return (color - a - u + 9) % 3
@@ -289,19 +369,38 @@
             send1.at[color, step - 1, w], recv1.at[color, step - 1, w], device(along(place, color, step), core))
 
     def each(function):
-        for color in range(3):
+        def go(w, _):
             for step in (2, 1, 3):
-                def go(w, _):
+                for color in range(3):
                     there, copies = first(color, step, w)
 
                     @pl.when(there)
                     def _():
                         for copy in copies:
                             function(copy)
-                    return 0
-                lax.fori_loop(0, 8, go, 0)
-
+            return 0
+        lax.fori_loop(0, 8, go, 0)
+
+    def own(color, w):
+        u = w // 2
+        v = least(color, place[color], u) + 3 * (w % 2)
+        chunk = jnp.minimum(number(color, place[color], u, v), 63)
+        return v <= 3, [pltpu.make_async_copy(o_ref.at[chunk], p0.at[color, w], own_sem.at[color, w, 0]),
+                        pltpu.make_async_copy(side_ref.at[chunk], p0s.at[color, w], own_sem.at[color, w, 1])]
+
+    def fetch(w, _):
+        for color in range(3):
+            there, copies = own(color, w)
+
+            @pl.when(there)
+            def _():
+                for copy in copies:
+                    copy.start()
+        return 0
+
+    greet(place, core)
     each(lambda copy: copy.start())
+    lax.fori_loop(0, 8, fetch, 0)
 
     def second(color, u, half):
         axis = (color + 1) % 3
@@ -314,10 +413,10 @@
 
     def fold(sources, target, target_side):
         for pair in range(2):
-            weighted, top, total = merge([(values[pair], side[pair]) for values, side in sources])
+            weighted, top, total = merge([(values[pair], side[pair * 4:pair * 4 + 4]) for values, side in sources])
             values, scale = encode(weighted)
             target[pair] = values
-            target_side[pair] = jnp.concatenate([top, total, scale, jnp.zeros((5, 128), jnp.float32)], axis=0)
+            target_side[pair * 4:pair * 4 + 4] = jnp.concatenate([top, total, scale, scale], axis=0)
 
     for color in range(3):
         a = place[color]
@@ -332,8 +431,9 @@
                 for step in (1, 2, 3):
                     for copy in first(color, step, w)[1]:
                         copy.wait_recv()
-                chunk = jnp.minimum(number(color, a, u, v), 63)
-                fold([(o_ref.at[chunk], side_ref.at[chunk])]
+                for copy in own(color, w)[1]:
+                    copy.wait()
+                fold([(p0.at[color, w], p0s.at[color, w])]
                      + [(r1.at[color, k, w], r1s.at[color, k, w]) for k in range(3)],
                      p1.at[color, w], p1s.at[color, w])
 
@@ -383,7 +483,7 @@
     half = third_at // 3
     mine = [(p2.at[color, half], p2s.at[color, half])] + [(r3.at[k], r3s.at[k]) for k in range(3)]
     for pair in range(2):
-        weighted, top, total = merge([(values[pair], side[pair]) for values, side in mine])
+        weighted, top, total = merge([(values[pair], side[pair * 4:pair * 4 + 4]) for values, side in mine])
         done = jnp.transpose(weighted / total)
         for g in range(2):
             for owner in range(2):
@@ -425,36 +525,32 @@
 
 
 def merge_parts(values, side):
-    vmem = pl.BlockSpec(memory_space=pltpu.VMEM)
+    hbm, vmem = pl.BlockSpec(memory_space=pl.ANY), pl.BlockSpec(memory_space=pltpu.VMEM)
     dma = pltpu.SemaphoreType.DMA
 
     def both(*lead):
-        return [pltpu.VMEM((*lead, 2, 128, 128), jnp.int16), pltpu.VMEM((*lead, 2, 8, 128), jnp.float32)]
+        return [pltpu.VMEM((*lead, 2, 128, 128), jnp.int16), pltpu.VMEM((*lead, 8, 128), jnp.float32)]
 
     return pl.pallas_call(
         merge_kernel,
         out_shape=jax.ShapeDtypeStruct((4, 64, 128), jnp.bfloat16),
-        in_specs=[vmem, vmem],
+        in_specs=[hbm, hbm],
         out_specs=vmem,
         scratch_shapes=[
-            *both(3, 3, 8), *both(3, 8), *both(3, 3, 2), *both(3, 2), *both(3),
+            *both(3, 8), *both(3, 3, 8), *both(3, 8), *both(3, 3, 2), *both(3, 2), *both(3),
             pltpu.VMEM((2, 4, 32, 128), jnp.float32), pltpu.VMEM((4, 32, 128), jnp.float32), pltpu.VMEM((4, 64, 128), jnp.float32),
-            dma((3, 3, 8, 2)), dma((3, 3, 8, 2)), dma((3, 3, 2, 2)), dma((3, 3, 2, 2)), dma((3, 3, 2)), dma((3, 2)), dma((2,)),
+            dma((3, 3, 8, 2)), dma((3, 3, 8, 2)), dma((3, 3, 2, 2)), dma((3, 3, 2, 2)), dma((3, 3, 2)), dma((3, 2)), dma((2,)), dma((3, 8, 2)),
         ],
-        compiler_params=pltpu.CompilerParams(collective_id=1, has_side_effects=True, vmem_limit_bytes=48 * 2**20),
+        compiler_params=pltpu.CompilerParams(collective_id=1, has_side_effects=True, vmem_limit_bytes=62 * 2**20),
         name="merge_parts",
     )(values, side)
 
 
 def local(queries, suffix_k, suffix_v, pool_k, pool_v, list_holder, list_slot, list_valid):
-    lists = jnp.zeros((8, 128), jnp.int32).at[0:3, 0:8].set(jnp.stack([list_holder[:, 0], list_slot, list_valid]))
-    gathered, every_list = gather_queries(queries, lists)
-    keys = jnp.transpose(pool_k, (0, 2, 1, 3))
-    values = jnp.transpose(pool_v, (0, 2, 3, 1))
-    near_k = jnp.pad(jnp.transpose(suffix_k, (1, 0, 2)), ((0, 0), (0, 8), (0, 0)))
-    near_v = jnp.concatenate([jnp.transpose(suffix_v, (1, 2, 0)), jnp.ones((4, 16, 8), jnp.bfloat16)], axis=1)
-    near_v = jnp.pad(near_v, ((0, 0), (0, 0), (0, 120)))
-    parts, side = attend(every_list, gathered.reshape(64, 256, 128), keys, values, near_k, near_v)
+    pool_k, pool_v = pool_k.reshape(16, 1024, 128), pool_v.reshape(16, 1024, 128)
+    gathered, lists, keys, values = gather_queries(queries, list_holder.reshape(8), list_slot, list_valid, pool_k, pool_v)
+    near = suffix_k.reshape(32, 128), suffix_v.reshape(32, 128)
+    parts, side = attend(lists, gathered.reshape(64, 256, 128), keys, values, *near)
     return merge_parts(parts, side)
 
 

time: 191 us -> 154 us (0.81)
  the two profiles are of different devices: /device:TPU:5 before, /device:TPU:17 now
where the time goes in v2:
time: 154 us
  Pallas kernels  152 us (99%)
    pallas_call x1, Pallas kernels, attend(): pl.pallas_call(attend_kernel, grid=(2,), in_specs=[pl.BlockSpec(memory_sp...  73.3 us
    pallas_call x1, Pallas kernels, merge_parts(): pl.pallas_call(merge_kernel, out_shape=jax.ShapeDtypeStruct((4, 64, 128),...  42.2 us
    pallas_call x1, Pallas kernels, gather_queries(): pl.pallas_call(gather_kernel, out_shape=[jax.ShapeDtypeStruct((4, 4, 4, 2...  37 us

profile of v2, /device:TPU:17, one launch (start us, length us, event | category | flops | bytes accessed | tf_op | source)
XLA Modules:
  0.0 153.9 jit_solution(7953956485640278642)
XLA Ops:
  0.0 37.0 %gather_queries.1 = (bf16[4,4,4,256,128]{4,3,2,1,0:T(8,128)(2,1)}, s32[4,8,128]{2,1,0:T(8,128)}, bf16[16,4,256,128]{3,2,1,0:T(8,128)(2,1)}, bf16[16,4,128,256]{3,2,1,0:T(8,128)(2,1)}) custom-call(bf16[4,64,128]{2,1,0:T(8,128)(2,1)} %q_ref.1, s32[8]{0:T(128)} %bitcast.11, s32[8]{0:T(128)} %slot_ref.1, s32[8]{0:T(128)} %valid_ref.1, ...), custom_call_target="tpu_custom_call" | custom-call | tf_op jit(solution)/shard_map/gather_queries/pallas_call | solution.py:164
  37.0 73.3 %attend.1 = (s16[64,2,128,128]{3,2,1,0:T(8,128)(2,1)}, f32[64,8,128]{2,1,0:T(8,128)}) custom-call(s32[4,8,128]{2,1,0:T(8,128)} %get-tuple-element.11.list_ref, bf16[64,256,128]{2,1,0:T(8,128)(2,1)} %bitcast.6, bf16[16,4,256,128]{3,2,1,0:T(8,128)(2,1)} %get-tuple-element.13.pk_ref, bf16[16,4,128,256]{3,2,1,0:T(8,128)(2,1)} %get-tuple-element.14.pv_ref, ...), custom_call_target="tpu_custom_call" | custom-call | tf_op jit(solution)/shard_map/attend/pallas_call | solution.py:310
  110.3 42.2 %merge_parts.1 = bf16[4,64,128]{2,1,0:T(8,128)(2,1)} custom-call(s16[64,2,128,128]{3,2,1,0:T(8,128)(2,1)} %get-tuple-element.15.o_ref, f32[64,8,128]{2,1,0:T(8,128)} %get-tuple-element.16.side_ref), custom_call_target="tpu_custom_call" | custom-call | tf_op jit(solution)/shard_map/merge_parts/pallas_call | solution.py:534
  152.5 1.5 copy.10

commit v3 on v2

--- a/solution.py
+++ b/solution.py
@@ -13,8 +13,10 @@
 NT = (((1,), (1,)), ((), ()))
 NN = (((1,), (0,)), ((), ()))
 MESH = pl.DeviceIdType.MESH
-PARTS = ((0, 80), (80, 80), (160, 96))
+PARTS = ((0, 48, 32), (80, 32, 48), (160, 48, 48))
+SPLIT = ((0, 1, 0, 80), (1, 1, 0, 80), (0, 2, 80, 48))
 JOBS = 12
+SIZES = (256, 192, 128)
 TOP16 = 32767.0
 
 
@@ -114,38 +116,45 @@
     keep = pltpu.make_async_copy(own, all_ref.at[place[0], place[1], place[2]], own_sem.at[0])
     keep.start()
 
-    def copies(part, phase):
+    def links(part, phase):
         order = [(part + i) % 3 for i in range(3)]
-        rows = pl.ds(*PARTS[part])
-        where = [slice(None) if axis in order[:phase] else place[axis] for axis in range(3)]
-        block = all_ref.at[where[0], where[1], where[2], rows]
-        source = own.at[rows] if phase == 0 else block
-        return [
-            pltpu.make_async_remote_copy(
-                source, block, send_sem.at[part, phase, step - 1], recv_sem.at[part, phase, step - 1],
-                device_id=device(along(place, order[phase], step), core), device_id_type=MESH)
-            for step in (1, 2, 3)
-        ]
-
-    started = []
+        axis, (at, upper, lower) = order[phase], PARTS[part]
+        halves = pl.ds(at, upper), pl.ds(at + upper, lower)
+        plan = ((0, 1, 0), (1, 3, 0), (1, 1, 0), (0, 3, 0), (0, 1, 3), (1, 3, 1))
+        copies = []
+        for i, (half, step, origin) in enumerate(plan):
+            source = along(place, axis, origin)
+            where = [slice(None) if d in order[:phase] else source[d] for d in range(3)]
+            block = all_ref.at[where[0], where[1], where[2], halves[half]]
+            copies.append(pltpu.make_async_remote_copy(
+                own.at[halves[half]] if phase == 0 and origin == 0 else block, block,
+                send_sem.at[part, phase, i], recv_sem.at[part, phase, i],
+                device_id=device(along(place, axis, step), core), device_id_type=MESH))
+        return copies
+
     for phase in range(3):
         for part in range(3):
             if phase:
-                for copy in started[(phase - 1) * 3 + part]:
-                    copy.wait_recv()
+                for i in (2, 3, 4, 5):
+                    links(part, phase - 1)[i].wait_recv()
             if phase == 1 and part == 0:
                 keep.wait()
-            now = copies(part, phase)
-            for copy in now:
+            for copy in links(part, phase)[:4]:
                 copy.start()
-            started.append(now)
-        over(*((0, 3), (3, 7), (7, 16))[phase], regroup)
-    for part in range(3):
-        for copy in started[6 + part]:
-            copy.wait_recv()
-    for group in started:
-        for copy in group:
-            copy.wait_send()
+        over(*((0, 1), (2, 4), (6, 10))[phase], regroup)
+        for part in range(3):
+            now = links(part, phase)
+            for i in (0, 1):
+                now[i].wait_recv()
+                now[i + 4].start()
+        over(*((1, 2), (4, 6), (10, 16))[phase], regroup)
+    for part in range(3):
+        for i in (2, 3, 4, 5):
+            links(part, 2)[i].wait_recv()
+    for part in range(3):
+        for phase in range(3):
+            for copy in links(part, phase):
+                copy.wait_send()
     for copy in lists:
         copy.wait()
     own_lists.wait()
@@ -175,7 +184,7 @@
             pltpu.VMEM((16, 1024, 128), jnp.bfloat16), pltpu.VMEM((16, 1024, 128), jnp.bfloat16),
             pltpu.VMEM((16, 4, 256, 128), jnp.bfloat16), pltpu.VMEM((16, 4, 128, 256), jnp.bfloat16),
             pltpu.VMEM((1024, 128), jnp.float32), pltpu.VMEM((1024, 128), jnp.float32),
-            dma((2,)), dma((2, 3)), dma((2,)), dma((3, 3, 3)), dma((3, 3, 3)), dma((2, 16)), dma((2, 16)),
+            dma((2,)), dma((2, 3)), dma((2,)), dma((3, 3, 6)), dma((3, 3, 6)), dma((2, 16)), dma((2, 16)),
         ],
         compiler_params=pltpu.CompilerParams(collective_id=0, has_side_effects=True, vmem_limit_bytes=62 * 2**20),
         name="gather_queries",
@@ -187,8 +196,8 @@
     @pl.when(pl.program_id(0) == 0)
     def prepare():
         store = lax.axis_index("store")
-        count[0] = 0
-        count[1] = 0
+        for i in range(len(SIZES)):
+            count[i] = 0
 
         def look(i, _):
             row, e = i // 8, i % 8
@@ -196,12 +205,11 @@
 
             @pl.when((list_ref[row, 0, e] == store) & (valid > 0))
             def _():
-                long = valid > 128
-                n = jnp.where(long, count[0], JOBS - 1 - count[1])
+                size = jnp.where(valid > SIZES[1], 0, jnp.where(valid > SIZES[2], 1, 2))
+                n = size * JOBS + count[size]
                 jobs[0, n] = slot
                 jobs[1, n] = valid
-                count[0] = count[0] + jnp.where(long, 1, 0)
-                count[1] = count[1] + jnp.where(long, 0, 1)
+                count[size] = count[size] + 1
                 pltpu.make_async_copy(pk_ref.at[slot], kj.at[n], sem.at[0, n]).start()
                 pltpu.make_async_copy(pv_ref.at[slot], vj.at[n, :, 0:128], sem.at[1, n]).start()
             return 0
@@ -229,8 +237,8 @@
                 vj[n, g, 128:144] = live_lane[0:16].astype(jnp.float32).astype(jnp.bfloat16)
             return 0
 
-        lax.fori_loop(0, count[0], fix, 0)
-        lax.fori_loop(JOBS - count[1], JOBS, fix, 0)
+        for i in range(len(SIZES)):
+            lax.fori_loop(i * JOBS, i * JOBS + count[i], fix, 0)
 
     pair = pl.program_id(0)
     suffix_at = (lax.axis_index("store") * 16 + lax.axis_index("ctx")) * 8
@@ -272,11 +280,10 @@
 
             lax.fori_loop(0, many, go, 0)
 
-        long, short = count[0], count[1]
-        units(0, long // 2, 2, 256)
-        units(long - long % 2, long % 2, 1, 256)
-        units(JOBS - short, short // 2, 2, 128)
-        units(JOBS - 1, short % 2, 1, 128)
+        for i, keys in enumerate(SIZES):
+            many = count[i]
+            units(i * JOBS, many // 2, 2, keys)
+            units(i * JOBS + many - many % 2, many % 2, 1, keys)
 
     low = lax.broadcasted_iota(jnp.int32, (1, 128), 1) < 64
 
@@ -296,7 +303,7 @@
             side_ref[i * 2 + odd, pl.ds(pair * 4, 4), :] = jnp.concatenate([top, whole[128:129], scale, scale], axis=0)
         return 0
 
-    lax.fori_loop(0, 32, emit, 0)
+    lax.fori_loop(0, 32, emit, 0, unroll=8)
 
 
 def encode(x):
@@ -320,10 +327,10 @@
         out_specs=[pl.BlockSpec((64, 1, 128, 128), lambda i: (0, i, 0, 0)), pl.BlockSpec((64, 8, 128), lambda i: (0, 0, 0))],
         out_shape=[jax.ShapeDtypeStruct((64, 2, 128, 128), jnp.int16), jax.ShapeDtypeStruct((64, 8, 128), jnp.float32)],
         scratch_shapes=[
-            pltpu.VMEM((JOBS, 4, 256, 128), jnp.bfloat16), pltpu.VMEM((JOBS, 4, 144, 256), jnp.bfloat16),
+            pltpu.VMEM((3 * JOBS, 4, 256, 128), jnp.bfloat16), pltpu.VMEM((3 * JOBS, 4, 144, 256), jnp.bfloat16),
             pltpu.VMEM((4, 16, 128), jnp.bfloat16), pltpu.VMEM((4, 144, 128), jnp.bfloat16), pltpu.VMEM((2, 32, 128), jnp.float32),
             pltpu.VMEM((2, 1, 4096), jnp.float32), pltpu.VMEM((2, 144, 4096), jnp.float32),
-            pltpu.SMEM((2, JOBS), jnp.int32), pltpu.SMEM((2,), jnp.int32), pltpu.SemaphoreType.DMA((2, JOBS)),
+            pltpu.SMEM((2, 3 * JOBS), jnp.int32), pltpu.SMEM((3,), jnp.int32), pltpu.SemaphoreType.DMA((2, 3 * JOBS)),
         ],
         compiler_params=pltpu.CompilerParams(vmem_limit_bytes=62 * 2**20),
         name="attend",
@@ -340,151 +347,105 @@
     return weighted, top, total
 
 
-def merge_kernel(o_ref, side_ref, out_ref, p0, p0s, r1, r1s, p1, p1s, r2, r2s, p2, p2s, r3, r3s, rows, swapped, wide,
-                 send1, recv1, send2, recv2, send3, recv3, swap_sem, own_sem):
+def merge_kernel(o_ref, side_ref, out_ref, *scratch):
+    buffers = [scratch[i * 12:(i + 1) * 12] for i in range(3)]
+    rows, swapped, wide, send_sem, recv_sem, own_sem, swap_sem = scratch[36:]
     place, core = position()
 
-    def least(color, a, u):
-        return (color - a - u + 9) % 3
-
-    def number(color, a, u, v):
-        at = [None] * 3
-        for axis, value in zip([(color + i) % 3 for i in range(3)], (a, u, v)):
-            at[axis] = value
-        return at[0] * 16 + at[1] * 4 + at[2]
-
-    def two(source, source_side, target, target_side, send, recv, to):
+    def cut(part, at):
+        pair, pairs, row, many = SPLIT[part]
+        where = [slice(None)] * 3
+        where[part] = at
+        return (o_ref.at[where[0], where[1], where[2], pl.ds(pair, pairs), pl.ds(row, many)],
+                side_ref.at[where[0], where[1], where[2]])
+
+    def line(part, ref, at, other=slice(None)):
+        return ref.at[other, at] if part == 1 else ref.at[at, other]
+
+    def copies(part, stage, step):
+        p0, p0s, r1, r1s, m1, m1s, r2, r2s, m2, m2s, r3, r3s = buffers[part]
+        axis = (part + stage) % 3
+        to = along(place, axis, step)
+        if stage == 0:
+            sources, targets = cut(part, to[axis]), (r1, r1s)
+        elif stage == 1:
+            sources, targets = (line(part, m1, to[axis]), line(part, m1s, to[axis])), (r2, r2s)
+        else:
+            sources, targets = (m2.at[to[axis]], m2s.at[to[axis]]), (r3, r3s)
         return [
-            pltpu.make_async_remote_copy(source, target, send.at[0], recv.at[0], device_id=to, device_id_type=MESH),
-            pltpu.make_async_remote_copy(source_side, target_side, send.at[1], recv.at[1], device_id=to, device_id_type=MESH),
+            pltpu.make_async_remote_copy(
+                source, target.at[step - 1], send_sem.at[part, stage, step - 1, i], recv_sem.at[part, stage, step - 1, i],
+                device_id=device(to, core), device_id_type=MESH)
+            for i, (source, target) in enumerate(zip(sources, targets))
         ]
 
-    def first(color, step, w):
-        a = (place[color] + step) % 4
-        u = w // 2
-        v = least(color, a, u) + 3 * (w % 2)
-        chunk = jnp.minimum(number(color, a, u, v), 63)
-        return v <= 3, two(
-            o_ref.at[chunk], side_ref.at[chunk], r1.at[color, step - 1, w], r1s.at[color, step - 1, w],
-            send1.at[color, step - 1, w], recv1.at[color, step - 1, w], device(along(place, color, step), core))
-
-    def each(function):
-        def go(w, _):
-            for step in (2, 1, 3):
-                for color in range(3):
-                    there, copies = first(color, step, w)
-
-                    @pl.when(there)
-                    def _():
-                        for copy in copies:
-                            function(copy)
+    def start(part, stage):
+        for step in (2, 1, 3):
+            for copy in copies(part, stage, step):
+                copy.start()
+
+    def arrive(part, stage):
+        for step in (1, 2, 3):
+            for copy in copies(part, stage, step):
+                copy.wait_recv()
+
+    def combine(part, sources):
+        pair, pairs = SPLIT[part][:2]
+        return [merge([(values[i], side[(pair + i) * 4:(pair + i) * 4 + 4]) for values, side in sources]) for i in range(pairs)]
+
+    def fold(part, sources, target, target_side):
+        pair = SPLIT[part][0]
+        sides = [jnp.zeros((4, 128), jnp.float32)] * 2
+        for i, (weighted, top, total) in enumerate(combine(part, sources)):
+            values, scale = encode(weighted)
+            target[i] = values
+            sides[pair + i] = jnp.concatenate([top, total, scale, scale], axis=0)
+        target_side[...] = jnp.concatenate(sides, axis=0)
+
+    keep = [[pltpu.make_async_copy(source, target, own_sem.at[part, i])
+             for i, (source, target) in enumerate(zip(cut(part, place[part]), buffers[part][:2]))] for part in range(3)]
+    for pair in keep:
+        for copy in pair:
+            copy.start()
+    greet(place, core)
+    for part in range(3):
+        start(part, 0)
+    for part in range(3):
+        p0, p0s, r1, r1s, m1, m1s = buffers[part][:6]
+        for copy in keep[part]:
+            copy.wait()
+        arrive(part, 0)
+
+        def first(n, _):
+            i, j = n // 4, n % 4
+            fold(part, [(p0.at[i, j], p0s.at[i, j])] + [(r1.at[k, i, j], r1s.at[k, i, j]) for k in range(3)],
+                 m1.at[i, j], m1s.at[i, j])
             return 0
-        lax.fori_loop(0, 8, go, 0)
-
-    def own(color, w):
-        u = w // 2
-        v = least(color, place[color], u) + 3 * (w % 2)
-        chunk = jnp.minimum(number(color, place[color], u, v), 63)
-        return v <= 3, [pltpu.make_async_copy(o_ref.at[chunk], p0.at[color, w], own_sem.at[color, w, 0]),
-                        pltpu.make_async_copy(side_ref.at[chunk], p0s.at[color, w], own_sem.at[color, w, 1])]
-
-    def fetch(w, _):
-        for color in range(3):
-            there, copies = own(color, w)
-
-            @pl.when(there)
-            def _():
-                for copy in copies:
-                    copy.start()
-        return 0
-
-    greet(place, core)
-    each(lambda copy: copy.start())
-    lax.fori_loop(0, 8, fetch, 0)
-
-    def second(color, u, half):
-        axis = (color + 1) % 3
-        step = (u - place[axis] + 4) % 4
-        to = list(place)
-        to[axis] = u
-        at = jnp.maximum(step - 1, 0)
-        return two(p1.at[color, u * 2 + half], p1s.at[color, u * 2 + half], r2.at[color, at, half], r2s.at[color, at, half],
-                   send2.at[color, at, half], recv2.at[color, at, half], device(to, core))
-
-    def fold(sources, target, target_side):
-        for pair in range(2):
-            weighted, top, total = merge([(values[pair], side[pair * 4:pair * 4 + 4]) for values, side in sources])
-            values, scale = encode(weighted)
-            target[pair] = values
-            target_side[pair * 4:pair * 4 + 4] = jnp.concatenate([top, total, scale, scale], axis=0)
-
-    for color in range(3):
-        a = place[color]
-        second_at = place[(color + 1) % 3]
-
-        def go(w, _):
-            u = w // 2
-            v = least(color, a, u) + 3 * (w % 2)
-
-            @pl.when(v <= 3)
-            def _():
-                for step in (1, 2, 3):
-                    for copy in first(color, step, w)[1]:
-                        copy.wait_recv()
-                for copy in own(color, w)[1]:
-                    copy.wait()
-                fold([(p0.at[color, w], p0s.at[color, w])]
-                     + [(r1.at[color, k, w], r1s.at[color, k, w]) for k in range(3)],
-                     p1.at[color, w], p1s.at[color, w])
-
-                @pl.when(u != second_at)
-                def _():
-                    for copy in second(color, u, w % 2):
-                        copy.start()
+
+        lax.fori_loop(0, 16, first, 0)
+        start(part, 1)
+    for part in range(3):
+        m1, m1s, r2, r2s, m2, m2s = buffers[part][4:10]
+        at = place[(part + 1) % 3]
+        arrive(part, 1)
+
+        def second(c, _):
+            fold(part, [(line(part, m1, at, c), line(part, m1s, at, c))] + [(r2.at[k, c], r2s.at[k, c]) for k in range(3)],
+                 m2.at[c], m2s.at[c])
             return 0
 
-        lax.fori_loop(0, 8, go, 0)
-
-    def third(color, half, v):
-        axis = (color + 2) % 3
-        at = jnp.maximum((v - place[axis] + 4) % 4 - 1, 0)
-        to = list(place)
-        to[axis] = v
-        return two(p2.at[color, half], p2s.at[color, half], r3.at[at], r3s.at[at],
-                   send3.at[color, at], recv3.at[at], device(to, core))
-
-    for color in range(3):
-        a, b, c = place[color], place[(color + 1) % 3], place[(color + 2) % 3]
-        for half in range(2):
-            v = least(color, a, b) + 3 * half
-
-            @pl.when(v <= 3)
-            def _():
-                for k in range(3):
-                    for copy in two(p1.at[color, 0], p1s.at[color, 0], r2.at[color, k, half], r2s.at[color, k, half],
-                                    send2.at[color, k, half], recv2.at[color, k, half], device(along(place, (color + 1) % 3, 1), core)):
-                        copy.wait_recv()
-                slot = b * 2 + half
-                fold([(p1.at[color, slot], p1s.at[color, slot])]
-                     + [(r2.at[color, k, half], r2s.at[color, k, half]) for k in range(3)],
-                     p2.at[color, half], p2s.at[color, half])
-
-                @pl.when(v != c)
-                def _():
-                    for copy in third(color, half, v):
-                        copy.start()
-
-    color = (place[0] + place[1] + place[2]) % 3
-    for k in range(3):
-        for copy in two(p2.at[0, 0], p2s.at[0, 0], r3.at[k], r3s.at[k], send3.at[0, k], recv3.at[k],
-                        device(along(place, 0, 1), core)):
-            copy.wait_recv()
-    third_at = jnp.where(color == 0, place[2], jnp.where(color == 1, place[0], place[1]))
-    half = third_at // 3
-    mine = [(p2.at[color, half], p2s.at[color, half])] + [(r3.at[k], r3s.at[k]) for k in range(3)]
+        lax.fori_loop(0, 4, second, 0)
+        start(part, 2)
+    pieces = [[], []]
+    for part in range(3):
+        m2, m2s, r3, r3s = buffers[part][8:]
+        at = place[(part + 2) % 3]
+        arrive(part, 2)
+        sources = [(m2.at[at], m2s.at[at])] + [(r3.at[k], r3s.at[k]) for k in range(3)]
+        for i, (weighted, _, total) in enumerate(combine(part, sources)):
+            pieces[SPLIT[part][0] + i].append(weighted / total)
     for pair in range(2):
-        weighted, top, total = merge([(values[pair], side[pair * 4:pair * 4 + 4]) for values, side in mine])
-        done = jnp.transpose(weighted / total)
+        done = jnp.transpose(jnp.concatenate(pieces[pair], axis=0))
         for g in range(2):
             for owner in range(2):
                 rows[owner, pair * 2 + g] = done[g * 64 + owner * 32:g * 64 + (owner + 1) * 32]
@@ -501,49 +462,33 @@
     wide[:, pl.ds(pl.multiple_of((1 - core) * 32, 32), 32), :] = tokens(swapped[...])
     out_ref[...] = wide[...].astype(jnp.bfloat16)
 
-    each(lambda copy: copy.wait_send())
-    for color in range(3):
-        a, b, c = place[color], place[(color + 1) % 3], place[(color + 2) % 3]
-
-        def go(w, _):
-            u = w // 2
-
-            @pl.when((least(color, a, u) + 3 * (w % 2) <= 3) & (u != b))
-            def _():
-                for copy in second(color, u, w % 2):
-                    copy.wait_send()
-            return 0
-
-        lax.fori_loop(0, 8, go, 0)
-        for half in range(2):
-            v = least(color, a, b) + 3 * half
-
-            @pl.when((v <= 3) & (v != c))
-            def _():
-                for copy in third(color, half, v):
+    for part in range(3):
+        for stage in range(3):
+            for step in (1, 2, 3):
+                for copy in copies(part, stage, step):
                     copy.wait_send()
 
 
 def merge_parts(values, side):
     hbm, vmem = pl.BlockSpec(memory_space=pl.ANY), pl.BlockSpec(memory_space=pltpu.VMEM)
     dma = pltpu.SemaphoreType.DMA
-
-    def both(*lead):
-        return [pltpu.VMEM((*lead, 2, 128, 128), jnp.int16), pltpu.VMEM((*lead, 8, 128), jnp.float32)]
-
+    buffers = []
+    for _, pairs, _, many in SPLIT:
+        for lead in ((4, 4), (3, 4, 4), (4, 4), (3, 4), (4,), (3,)):
+            buffers += [pltpu.VMEM((*lead, pairs, many, 128), jnp.int16), pltpu.VMEM((*lead, 8, 128), jnp.float32)]
     return pl.pallas_call(
         merge_kernel,
         out_shape=jax.ShapeDtypeStruct((4, 64, 128), jnp.bfloat16),
         in_specs=[hbm, hbm],
         out_specs=vmem,
         scratch_shapes=[
-            *both(3, 8), *both(3, 3, 8), *both(3, 8), *both(3, 3, 2), *both(3, 2), *both(3),
+            *buffers,
             pltpu.VMEM((2, 4, 32, 128), jnp.float32), pltpu.VMEM((4, 32, 128), jnp.float32), pltpu.VMEM((4, 64, 128), jnp.float32),
-            dma((3, 3, 8, 2)), dma((3, 3, 8, 2)), dma((3, 3, 2, 2)), dma((3, 3, 2, 2)), dma((3, 3, 2)), dma((3, 2)), dma((2,)), dma((3, 8, 2)),
+            dma((3, 3, 3, 2)), dma((3, 3, 3, 2)), dma((3, 2)), dma((2,)),
         ],
         compiler_params=pltpu.CompilerParams(collective_id=1, has_side_effects=True, vmem_limit_bytes=62 * 2**20),
         name="merge_parts",
-    )(values, side)
+    )(values.reshape(4, 4, 4, 2, 128, 128), side.reshape(4, 4, 4, 8, 128))
 
 
 def local(queries, suffix_k, suffix_v, pool_k, pool_v, list_holder, list_slot, list_valid):

time: 154 us -> 146 us (0.948)
  the two profiles are of different devices: /device:TPU:17 before, /device:TPU:1 now
where the time goes in v3:
time: 146 us
  Pallas kernels  145 us (99%)
  local copies, waits for them, and re-layouts  1.47 us (1%)
    pallas_call x1, Pallas kernels, merge_parts(): pl.pallas_call(merge_kernel, out_shape=jax.ShapeDtypeStruct((4, 64, 128),...  81 us
    pallas_call x1, Pallas kernels, gather_queries(): pl.pallas_call(gather_kernel, out_shape=[jax.ShapeDtypeStruct((4, 4, 4, 2...  35.9 us
    pallas_call x1, Pallas kernels, attend(): pl.pallas_call(attend_kernel, grid=(2,), in_specs=[pl.BlockSpec(memory_sp...  27.7 us

profile of v3, /device:TPU:1, one launch (start us, length us, event | category | flops | bytes accessed | tf_op | source)
XLA Modules:
  0.0 146.2 jit_solution(14290775304383909236)
XLA Ops:
  0.0 35.9 %gather_queries.1 = (bf16[4,4,4,256,128]{4,3,2,1,0:T(8,128)(2,1)}, s32[4,8,128]{2,1,0:T(8,128)}, bf16[16,4,256,128]{3,2,1,0:T(8,128)(2,1)}, bf16[16,4,128,256]{3,2,1,0:T(8,128)(2,1)}) custom-call(bf16[4,64,128]{2,1,0:T(8,128)(2,1)} %q_ref.1, s32[8]{0:T(128)} %bitcast.15, s32[8]{0:T(128)} %slot_ref.1, s32[8]{0:T(128)} %valid_ref.1, ...), custom_call_target="tpu_custom_call" | custom-call | tf_op jit(solution)/shard_map/gather_queries/pallas_call | solution.py:173
  36.0 27.7 %attend.1 = (s16[64,2,128,128]{3,2,1,0:T(8,128)(2,1)}, f32[64,8,128]{2,1,0:T(8,128)}) custom-call(s32[4,8,128]{2,1,0:T(8,128)} %get-tuple-element.11.list_ref, bf16[64,256,128]{2,1,0:T(8,128)(2,1)} %bitcast.8, bf16[16,4,256,128]{3,2,1,0:T(8,128)(2,1)} %get-tuple-element.13.pk_ref, bf16[16,4,128,256]{3,2,1,0:T(8,128)(2,1)} %get-tuple-element.14.pv_ref, ...), custom_call_target="tpu_custom_call" | custom-call | tf_op jit(solution)/shard_map/attend/pallas_call | solution.py:317
  63.7 81.0 %merge_parts.1 = bf16[4,64,128]{2,1,0:T(8,128)(2,1)} custom-call(s16[4,4,4,2,128,128]{5,4,3,2,1,0:T(8,128)(2,1)} %bitcast.11, f32[4,4,4,8,128]{4,3,2,1,0:T(8,128)} %bitcast.12), custom_call_target="tpu_custom_call" | custom-call | tf_op jit(solution)/shard_map/merge_parts/pallas_call | solution.py:479
  144.8 1.5 %copy.10 = bf16[4,64,128]{2,1,0:T(8,128)(2,1)} copy(bf16[4,64,128]{2,1,0:T(8,128)(2,1)} %merge_parts.1) | data formatting | bytes 131072

commit v4 on v3

--- a/solution.py
+++ b/solution.py
@@ -13,9 +13,11 @@
 NT = (((1,), (1,)), ((), ()))
 NN = (((1,), (0,)), ((), ()))
 MESH = pl.DeviceIdType.MESH
-PARTS = ((0, 48, 32), (80, 32, 48), (160, 48, 48))
+PARTS = ((0, 48, 48), (96, 32, 32), (160, 48, 48))
 SPLIT = ((0, 1, 0, 80), (1, 1, 0, 80), (0, 2, 80, 48))
-JOBS = 12
+ORDERS = ((0, 1, 2), (1, 2, 0), (0, 2, 1))
+JOBS = 14
+COSTS = (115, 90, 72)
 SIZES = (256, 192, 128)
 TOP16 = 32767.0
 
@@ -48,9 +50,55 @@
     pl.semaphore_wait(barrier, 10)
 
 
-def gather_kernel(q_ref, holder_ref, slot_ref, valid_ref, pk_ref, pv_ref, all_ref, lists_ref, kp_ref, vp_ref,
-                  list_ref, theirs, send, own, raw_k, raw_v, keys, values, wide_k, wide_v,
-                  swap_sem, list_sem, own_sem, send_sem, recv_sem, raw_sem, out_sem):
+def size_class(valid):
+    return jnp.where(valid > SIZES[1], 0, jnp.where(valid > SIZES[2], 1, 2))
+
+
+def pick(options, index):
+    value = options[0]
+    for i in range(1, len(options)):
+        value = jnp.where(index == i, options[i], value)
+    return value
+
+
+def whole(reduce, x):
+    return reduce(reduce(x, axis=1, keepdims=True), axis=0, keepdims=True)
+
+
+def plan_moves(holder, valid, number):
+    live = (valid > 0) & (number >= 0)
+    size = size_class(valid)
+    cost = jnp.where(live, pick([jnp.full_like(valid, c) for c in COSTS], size), 0)
+    loads = [whole(jnp.sum, jnp.where(holder == s, cost, 0)) for s in range(4)]
+    none = jnp.full((1, 1), -1, jnp.int32)
+    moves = [[none, none] for _ in range(4)]
+    for _ in range(5):
+        most = functools.reduce(jnp.maximum, loads)
+        giver = jnp.where(loads[0] == most, 0, jnp.where(loads[1] == most, 1, jnp.where(loads[2] == most, 2, 3)))
+        ways = []
+        for way, step in enumerate((1, 3)):
+            free = pick([moves[s][way] for s in range(4)], giver) < 0
+            ways.append(jnp.where(free, pick(loads[step:] + loads[:step], giver), 1 << 20))
+        way = jnp.where(ways[0] <= ways[1], 0, 1)
+        least = jnp.minimum(ways[0], ways[1])
+        gone = [pick([moves[s][w] for s in range(4)], giver) for w in range(2)]
+        at = live & (holder == giver) & (number != gone[0]) & (number != gone[1])
+        found = [whole(jnp.max, jnp.where(at & (size == k), number, -1)) for k in range(3)]
+        entry, saved = none, jnp.zeros((1, 1), jnp.int32)
+        for k in (2, 1, 0):
+            helps = (found[k] >= 0) & (least + COSTS[k] < most)
+            entry, saved = jnp.where(helps, found[k], entry), jnp.where(helps, COSTS[k], saved)
+        for s in range(4):
+            takes = ((giver == (s + 3) % 4) & (way == 0)) | ((giver == (s + 1) % 4) & (way == 1))
+            loads[s] = loads[s] - jnp.where(giver == s, saved, 0) + jnp.where(takes, saved, 0)
+            for w in range(2):
+                moves[s][w] = jnp.where((giver == s) & (way == w) & (entry >= 0), entry, moves[s][w])
+    return moves
+
+
+def gather_kernel(q_ref, holder_ref, slot_ref, valid_ref, pk_ref, pv_ref, all_ref, lists_ref, kp_ref, vp_ref, plan_ref,
+                  list_ref, table, plan_tile, out_k, out_v, in_k, in_v, theirs, send, own, raw_k, raw_v, keys, values, wide_k, wide_v,
+                  swap_sem, list_sem, own_sem, send_sem, recv_sem, raw_sem, out_sem, plan_sem, move_send, move_recv):
     place, core = position()
 
     def raw_copies(n):
@@ -87,22 +135,20 @@
     lists = []
     for step in (1, 2, 3):
         copy = pltpu.make_async_remote_copy(
-            list_ref, lists_ref.at[place[0]], list_sem.at[0, step - 1], list_sem.at[1, step - 1],
+            list_ref, table.at[place[0]], list_sem.at[0, step - 1], list_sem.at[1, step - 1],
             device_id=device(along(place, 0, step), core), device_id_type=MESH)
         copy.start()
         lists.append(copy)
-    own_lists = pltpu.make_async_copy(list_ref, lists_ref.at[place[0]], own_sem.at[1])
+    own_lists = pltpu.make_async_copy(list_ref, table.at[place[0]], own_sem.at[1])
     own_lists.start()
 
     def grouped(tokens):
         wide = tokens.astype(jnp.float32).reshape(4, 4, 8, 128)
         return jnp.stack([wide[:, g].reshape(32, 128) for g in range(4)]).astype(jnp.bfloat16)
 
-    def regroup(n):
-        for copy in raw_copies(n):
-            copy.wait()
-        wide_k[...] = raw_k[n].astype(jnp.float32)
-        wide_v[...] = raw_v[n].astype(jnp.float32)
+    def regroup(n, of_k=raw_k, of_v=raw_v, first=0):
+        wide_k[...] = of_k[n - first].astype(jnp.float32)
+        wide_v[...] = of_v[n - first].astype(jnp.float32)
         for g in range(4):
             keys[n, g] = wide_k[pl.ds(g, 256, stride=4), :].astype(jnp.bfloat16)
             values[n, g] = jnp.transpose(wide_v[pl.ds(g, 256, stride=4), :]).astype(jnp.bfloat16)
@@ -116,13 +162,14 @@
     keep = pltpu.make_async_copy(own, all_ref.at[place[0], place[1], place[2]], own_sem.at[0])
     keep.start()
 
-    def links(part, phase):
-        order = [(part + i) % 3 for i in range(3)]
+    def links(part, phase, which):
+        order = ORDERS[part]
         axis, (at, upper, lower) = order[phase], PARTS[part]
         halves = pl.ds(at, upper), pl.ds(at + upper, lower)
         plan = ((0, 1, 0), (1, 3, 0), (1, 1, 0), (0, 3, 0), (0, 1, 3), (1, 3, 1))
         copies = []
-        for i, (half, step, origin) in enumerate(plan):
+        for i in which:
+            half, step, origin = plan[i]
             source = along(place, axis, origin)
             where = [slice(None) if d in order[:phase] else source[d] for d in range(3)]
             block = all_ref.at[where[0], where[1], where[2], halves[half]]
@@ -132,38 +179,79 @@
                 device_id=device(along(place, axis, step), core), device_id_type=MESH))
         return copies
 
+    def move(way):
+        to = device(along(place, 0, (1, 3)[way]), core)
+        return [
+            pltpu.make_async_remote_copy(source.at[way], target.at[way], move_send.at[way, i], move_recv.at[way, i],
+                                         device_id=to, device_id_type=MESH)
+            for i, (source, target) in enumerate(((out_k, in_k), (out_v, in_v)))
+        ]
+
+    def ready(n):
+        for copy in raw_copies(n):
+            copy.wait()
+
+    def balance():
+        for copy in lists:
+            copy.wait()
+        own_lists.wait()
+        pltpu.make_async_copy(table, lists_ref, plan_sem.at[0]).start()
+        over(0, 16, ready)
+        holder, slots, valid = (table[:, i, :] for i in range(3))
+        lanes = lax.broadcasted_iota(jnp.int32, (4, 128), 1)
+        number = jnp.where(lanes < 8, lax.broadcasted_iota(jnp.int32, (4, 128), 0) * 8 + lanes, -1)
+        moves = plan_moves(holder, valid, number)
+        given = [pick([moves[s][way] for s in range(4)], place[0]) for way in range(2)]
+        taken = [pick([moves[s][way] for s in range(4)], (place[0] + (3, 1)[way]) % 4) for way in range(2)]
+        for way in range(2):
+            slot = jnp.max(jnp.where((number == given[way]) & (number >= 0), slots, 0))
+            out_k[way] = raw_k[slot]
+            out_v[way] = raw_v[slot]
+            for copy in move(way):
+                copy.start()
+        first_row = row == 0
+        told = jnp.zeros((8, 128), jnp.int32)
+        for i, value in enumerate(given + taken):
+            told = jnp.where(first_row & (lane == i), value, told)
+        plan_tile[...] = told
+        pltpu.make_async_copy(plan_tile, plan_ref, plan_sem.at[1]).start()
+
     for phase in range(3):
         for part in range(3):
             if phase:
                 for i in (2, 3, 4, 5):
-                    links(part, phase - 1)[i].wait_recv()
+                    links(part, phase - 1, (i,))[0].wait_recv()
             if phase == 1 and part == 0:
                 keep.wait()
-            for copy in links(part, phase)[:4]:
+            for copy in links(part, phase, range(4)):
                 copy.start()
-        over(*((0, 1), (2, 4), (6, 10))[phase], regroup)
+        over(*((0, 0), (2, 4), (6, 10))[phase], regroup)
         for part in range(3):
-            now = links(part, phase)
             for i in (0, 1):
-                now[i].wait_recv()
-                now[i + 4].start()
-        over(*((1, 2), (4, 6), (10, 16))[phase], regroup)
+                links(part, phase, (i,))[0].wait_recv()
+                links(part, phase, (i + 4,))[0].start()
+        if phase == 0:
+            balance()
+        over(*((0, 2), (4, 6), (10, 16))[phase], regroup)
+    for way in range(2):
+        for copy in move(way):
+            copy.wait()
+    over(16, 18, functools.partial(regroup, of_k=in_k, of_v=in_v, first=16))
     for part in range(3):
         for i in (2, 3, 4, 5):
-            links(part, 2)[i].wait_recv()
+            links(part, 2, (i,))[0].wait_recv()
     for part in range(3):
         for phase in range(3):
-            for copy in links(part, phase):
+            for copy in links(part, phase, range(6)):
                 copy.wait_send()
-    for copy in lists:
-        copy.wait()
-    own_lists.wait()
+    pltpu.make_async_copy(plan_tile, plan_ref, plan_sem.at[1]).wait()
+    pltpu.make_async_copy(table, lists_ref, plan_sem.at[0]).wait()
 
     def finish(n):
         for copy in out_copies(n):
             copy.wait()
 
-    over(0, 16, finish)
+    over(0, 18, finish)
 
 
 def gather_queries(queries, holder, slot, valid, pool_k, pool_v):
@@ -174,45 +262,60 @@
         gather_kernel,
         out_shape=[
             jax.ShapeDtypeStruct((4, 4, 4, 256, 128), jnp.bfloat16), jax.ShapeDtypeStruct((4, 8, 128), jnp.int32),
-            jax.ShapeDtypeStruct((16, 4, 256, 128), jnp.bfloat16), jax.ShapeDtypeStruct((16, 4, 128, 256), jnp.bfloat16),
+            jax.ShapeDtypeStruct((18, 4, 256, 128), jnp.bfloat16), jax.ShapeDtypeStruct((18, 4, 128, 256), jnp.bfloat16),
+            jax.ShapeDtypeStruct((8, 128), jnp.int32),
         ],
         in_specs=[vmem, smem, smem, smem, hbm, hbm],
-        out_specs=[hbm] * 4,
+        out_specs=[hbm] * 5,
         scratch_shapes=[
-            pltpu.VMEM((8, 128), jnp.int32), pltpu.VMEM((4, 32, 128), jnp.bfloat16),
+            pltpu.VMEM((8, 128), jnp.int32), pltpu.VMEM((4, 8, 128), jnp.int32), pltpu.VMEM((8, 128), jnp.int32),
+            *[pltpu.VMEM((2, 1024, 128), jnp.bfloat16)] * 4, pltpu.VMEM((4, 32, 128), jnp.bfloat16),
             pltpu.VMEM((4, 64, 128), jnp.bfloat16), pltpu.VMEM((256, 128), jnp.bfloat16),
             pltpu.VMEM((16, 1024, 128), jnp.bfloat16), pltpu.VMEM((16, 1024, 128), jnp.bfloat16),
-            pltpu.VMEM((16, 4, 256, 128), jnp.bfloat16), pltpu.VMEM((16, 4, 128, 256), jnp.bfloat16),
+            pltpu.VMEM((18, 4, 256, 128), jnp.bfloat16), pltpu.VMEM((18, 4, 128, 256), jnp.bfloat16),
             pltpu.VMEM((1024, 128), jnp.float32), pltpu.VMEM((1024, 128), jnp.float32),
-            dma((2,)), dma((2, 3)), dma((2,)), dma((3, 3, 6)), dma((3, 3, 6)), dma((2, 16)), dma((2, 16)),
+            dma((2,)), dma((2, 3)), dma((2,)), dma((3, 3, 6)), dma((3, 3, 6)), dma((2, 16)), dma((2, 18)), dma((2,)), dma((2, 2)), dma((2, 2)),
         ],
         compiler_params=pltpu.CompilerParams(collective_id=0, has_side_effects=True, vmem_limit_bytes=62 * 2**20),
         name="gather_queries",
     )(queries, holder, slot, valid, pool_k, pool_v)
 
 
-def attend_kernel(list_ref, q_ref, pk_ref, pv_ref, near_k_ref, near_v_ref, o_ref, side_ref,
+def attend_kernel(list_ref, plan_ref, q_ref, pk_ref, pv_ref, near_k_ref, near_v_ref, o_ref, side_ref,
                   kj, vj, sk_ref, sv_ref, near, peak, acc, jobs, count, sem):
+    def starts(size):
+        return (0, JOBS, JOBS - count[2])[size]
+
     @pl.when(pl.program_id(0) == 0)
     def prepare():
         store = lax.axis_index("store")
         for i in range(len(SIZES)):
             count[i] = 0
 
+        def add(slot, valid):
+            size = size_class(valid)
+            n = jnp.where(size == 0, count[0], jnp.where(size == 1, JOBS + count[1], JOBS - 1 - count[2]))
+            jobs[0, n] = slot
+            jobs[1, n] = valid
+            count[size] = count[size] + 1
+            pltpu.make_async_copy(pk_ref.at[slot], kj.at[n], sem.at[0, n]).start()
+            pltpu.make_async_copy(pv_ref.at[slot], vj.at[n, :, 0:128], sem.at[1, n]).start()
+
         def look(i, _):
-            row, e = i // 8, i % 8
-            slot, valid = list_ref[row, 1, e], list_ref[row, 2, e]
-
-            @pl.when((list_ref[row, 0, e] == store) & (valid > 0))
+            r, e = i // 8, i % 8
+            kept = (i != plan_ref[0, 0]) & (i != plan_ref[0, 1])
+
+            @pl.when((list_ref[r, 0, e] == store) & (list_ref[r, 2, e] > 0) & kept)
             def _():
-                size = jnp.where(valid > SIZES[1], 0, jnp.where(valid > SIZES[2], 1, 2))
-                n = size * JOBS + count[size]
-                jobs[0, n] = slot
-                jobs[1, n] = valid
-                count[size] = count[size] + 1
-                pltpu.make_async_copy(pk_ref.at[slot], kj.at[n], sem.at[0, n]).start()
-                pltpu.make_async_copy(pv_ref.at[slot], vj.at[n, :, 0:128], sem.at[1, n]).start()
+                add(list_ref[r, 1, e], list_ref[r, 2, e])
             return 0
+
+        for way in range(2):
+            entry = plan_ref[0, 2 + way]
+
+            @pl.when(entry >= 0)
+            def _():
+                add(16 + way, list_ref[entry // 8, 2, entry % 8])
 
         lax.fori_loop(0, 32, look, 0)
         near[0] = near_k_ref[...].astype(jnp.float32)
@@ -237,8 +340,8 @@
                 vj[n, g, 128:144] = live_lane[0:16].astype(jnp.float32).astype(jnp.bfloat16)
             return 0
 
-        for i in range(len(SIZES)):
-            lax.fori_loop(i * JOBS, i * JOBS + count[i], fix, 0)
+        for i in range(3):
+            lax.fori_loop(starts(i), starts(i) + count[i], fix, 0)
 
     pair = pl.program_id(0)
     suffix_at = (lax.axis_index("store") * 16 + lax.axis_index("ctx")) * 8
@@ -282,8 +385,8 @@
 
         for i, keys in enumerate(SIZES):
             many = count[i]
-            units(i * JOBS, many // 2, 2, keys)
-            units(i * JOBS + many - many % 2, many % 2, 1, keys)
+            units(starts(i), many // 2, 2, keys)
+            units(starts(i) + many - many % 2, many % 2, 1, keys)
 
     low = lax.broadcasted_iota(jnp.int32, (1, 128), 1) < 64
 
@@ -312,12 +415,13 @@
     return whole, largest * (1.0 / TOP16)
 
 
-def attend(lists, gathered, pool_k, pool_v, suffix_k, suffix_v):
+def attend(lists, plan, gathered, pool_k, pool_v, suffix_k, suffix_v):
     hbm = pl.BlockSpec(memory_space=pl.ANY)
     return pl.pallas_call(
         attend_kernel,
         grid=(2,),
         in_specs=[
+            pl.BlockSpec(memory_space=pltpu.SMEM),
             pl.BlockSpec(memory_space=pltpu.SMEM),
             pl.BlockSpec((64, 128, 128), lambda i: (0, i, 0)),
             hbm, hbm,
@@ -327,14 +431,14 @@
         out_specs=[pl.BlockSpec((64, 1, 128, 128), lambda i: (0, i, 0, 0)), pl.BlockSpec((64, 8, 128), lambda i: (0, 0, 0))],
         out_shape=[jax.ShapeDtypeStruct((64, 2, 128, 128), jnp.int16), jax.ShapeDtypeStruct((64, 8, 128), jnp.float32)],
         scratch_shapes=[
-            pltpu.VMEM((3 * JOBS, 4, 256, 128), jnp.bfloat16), pltpu.VMEM((3 * JOBS, 4, 144, 256), jnp.bfloat16),
+            pltpu.VMEM((2 * JOBS, 4, 256, 128), jnp.bfloat16), pltpu.VMEM((2 * JOBS, 4, 144, 256), jnp.bfloat16),
             pltpu.VMEM((4, 16, 128), jnp.bfloat16), pltpu.VMEM((4, 144, 128), jnp.bfloat16), pltpu.VMEM((2, 32, 128), jnp.float32),
             pltpu.VMEM((2, 1, 4096), jnp.float32), pltpu.VMEM((2, 144, 4096), jnp.float32),
-            pltpu.SMEM((2, 3 * JOBS), jnp.int32), pltpu.SMEM((3,), jnp.int32), pltpu.SemaphoreType.DMA((2, 3 * JOBS)),
+            pltpu.SMEM((2, 2 * JOBS), jnp.int32), pltpu.SMEM((3,), jnp.int32), pltpu.SemaphoreType.DMA((2, 2 * JOBS)),
         ],
         compiler_params=pltpu.CompilerParams(vmem_limit_bytes=62 * 2**20),
         name="attend",
-    )(lists, gathered, pool_k, pool_v, suffix_k, suffix_v)
+    )(lists, plan, gathered, pool_k, pool_v, suffix_k, suffix_v)
 
 
 def merge(parts):
@@ -493,9 +597,9 @@
 
 def local(queries, suffix_k, suffix_v, pool_k, pool_v, list_holder, list_slot, list_valid):
     pool_k, pool_v = pool_k.reshape(16, 1024, 128), pool_v.reshape(16, 1024, 128)
-    gathered, lists, keys, values = gather_queries(queries, list_holder.reshape(8), list_slot, list_valid, pool_k, pool_v)
+    gathered, lists, keys, values, plan = gather_queries(queries, list_holder.reshape(8), list_slot, list_valid, pool_k, pool_v)
     near = suffix_k.reshape(32, 128), suffix_v.reshape(32, 128)
-    parts, side = attend(lists, gathered.reshape(64, 256, 128), keys, values, *near)
+    parts, side = attend(lists, plan, gathered.reshape(64, 256, 128), keys, values, *near)
     return merge_parts(parts, side)
 
 

time: 146 us -> 135 us (0.925)
  Pallas kernels: 145 us -> 133 us
    pallas_call x1, Pallas kernels: 81 us -> 55.7 us  [merge_parts(): pl.pallas_call(merge_kernel, out_shape=jax.ShapeDtypeStruct((4, 64, 128),...]
    pallas_call x1, Pallas kernels: 27.7 us -> 39.3 us  [attend(): pl.pallas_call(attend_kernel, grid=(2,), in_specs=[pl.BlockSpec(memory_sp...]
    pallas_call x1, Pallas kernels: 35.9 us -> 38 us  [gather_queries(): pl.pallas_call(gather_kernel, out_shape=[jax.ShapeDtypeStruct((4, 4, 4, 2...]
where the time goes in v4:
time: 135 us; the launch traced here: 134 us
  Pallas kernels  133 us (99%)
  local copies, waits for them, and re-layouts  1.47 us (1%)
    pallas_call x1, Pallas kernels, merge_parts(): pl.pallas_call(merge_kernel, out_shape=jax.ShapeDtypeStruct((4, 64, 128),...  55.7 us
    pallas_call x1, Pallas kernels, attend(): pl.pallas_call(attend_kernel, grid=(2,), in_specs=[pl.BlockSpec(memory_sp...  39.3 us
    pallas_call x1, Pallas kernels, gather_queries(): pl.pallas_call(gather_kernel, out_shape=[jax.ShapeDtypeStruct((4, 4, 4, 2...  38 us

profile of v4, /device:TPU:1, one launch (start us, length us, event | category | flops | bytes accessed | tf_op | source)
XLA Modules:
  0.0 134.5 jit_solution(11270711740585549352)
XLA Ops:
  0.0 38.0 %gather_queries.1 = (bf16[4,4,4,256,128]{4,3,2,1,0:T(8,128)(2,1)}, s32[4,8,128]{2,1,0:T(8,128)}, bf16[18,4,256,128]{3,2,1,0:T(8,128)(2,1)}, bf16[18,4,128,256]{3,2,1,0:T(8,128)(2,1)}, s32[8,128]{1,0:T(8,128)}) custom-call(bf16[4,64,128]{2,1,0:T(8,128)(2,1)} %q_ref.1, s32[8]{0:T(128)} %bitcast.15, s32[8]{0:T(128)} %slot_ref.1, s32[8]{0:T(128)} %valid_ref.1, ...), custom_call_target="tpu_custom_call" | custom-call | tf_op jit(solution)/shard_map/gather_queries/pallas_call | solution.py:261
  38.0 39.3 %attend.1 = (s16[64,2,128,128]{3,2,1,0:T(8,128)(2,1)}, f32[64,8,128]{2,1,0:T(8,128)}) custom-call(s32[4,8,128]{2,1,0:T(8,128)} %get-tuple-element.12.list_ref, s32[8,128]{1,0:T(8,128)} %get-tuple-element.13.plan_ref, bf16[64,256,128]{2,1,0:T(8,128)(2,1)} %bitcast.10, bf16[18,4,256,128]{3,2,1,0:T(8,128)(2,1)} %get-tuple-element.15.pk_ref, ...), custom_call_target="tpu_custom_call" | custom-call | tf_op jit(solution)/shard_map/attend/pallas_call | solution.py:420
  77.3 55.7 %merge_parts.1 = bf16[4,64,128]{2,1,0:T(8,128)(2,1)} custom-call(s16[4,4,4,2,128,128]{5,4,3,2,1,0:T(8,128)(2,1)} %bitcast.11, f32[4,4,4,8,128]{4,3,2,1,0:T(8,128)} %bitcast.12), custom_call_target="tpu_custom_call" | custom-call | tf_op jit(solution)/shard_map/merge_parts/pallas_call | solution.py:583
  133.0 1.5 %copy.10 = bf16[4,64,128]{2,1,0:T(8,128)(2,1)} copy(bf16[4,64,128]{2,1,0:T(8,128)(2,1)} %merge_parts.1) | data formatting | bytes 131072

commit v5 on v4

--- a/solution.py
+++ b/solution.py
@@ -452,33 +452,50 @@
 
 
 def merge_kernel(o_ref, side_ref, out_ref, *scratch):
-    buffers = [scratch[i * 12:(i + 1) * 12] for i in range(3)]
-    rows, swapped, wide, send_sem, recv_sem, own_sem, swap_sem = scratch[36:]
+    buffers = [scratch[i * 18:(i + 1) * 18] for i in range(3)]
+    rows, swapped, wide, send_sem, recv_sem, ring_send, ring_recv, own_sem, swap_sem = scratch[54:]
     place, core = position()
 
-    def cut(part, at):
+    def cut(part, at, half=None):
         pair, pairs, row, many = SPLIT[part]
         where = [slice(None)] * 3
         where[part] = at
+        if half is not None:
+            where[1 if part == 0 else 0] = pl.ds(half * 2, 2)
         return (o_ref.at[where[0], where[1], where[2], pl.ds(pair, pairs), pl.ds(row, many)],
                 side_ref.at[where[0], where[1], where[2]])
 
     def line(part, ref, at, other=slice(None)):
         return ref.at[other, at] if part == 1 else ref.at[at, other]
 
+    def ring(part, way, kind):
+        r1, r1s, _, _, rin, rins, rout, routs = buffers[part][2:10]
+        step = (1, 3)[way]
+        to = along(place, part, step)
+        if kind == 0:
+            sources, targets = cut(part, along(place, part, 2)[part], way), (rin.at[way], rins.at[way])
+        else:
+            half = 1 - way if kind == 1 else way
+            sources = cut(part, to[part], half) if kind == 1 else (rout.at[way], routs.at[way])
+            targets = r1.at[way, pl.ds(half * 2, 2)], r1s.at[way, pl.ds(half * 2, 2)]
+        return [
+            pltpu.make_async_remote_copy(
+                source, target, ring_send.at[part, way, kind, i], ring_recv.at[part, way, kind, i],
+                device_id=device(to, core), device_id_type=MESH)
+            for i, (source, target) in enumerate(zip(sources, targets))
+        ]
+
     def copies(part, stage, step):
-        p0, p0s, r1, r1s, m1, m1s, r2, r2s, m2, m2s, r3, r3s = buffers[part]
+        m1, m1s, r2, r2s, m2, m2s, r3, r3s = buffers[part][10:]
         axis = (part + stage) % 3
         to = along(place, axis, step)
-        if stage == 0:
-            sources, targets = cut(part, to[axis]), (r1, r1s)
-        elif stage == 1:
+        if stage == 1:
             sources, targets = (line(part, m1, to[axis]), line(part, m1s, to[axis])), (r2, r2s)
         else:
             sources, targets = (m2.at[to[axis]], m2s.at[to[axis]]), (r3, r3s)
         return [
             pltpu.make_async_remote_copy(
-                source, target.at[step - 1], send_sem.at[part, stage, step - 1, i], recv_sem.at[part, stage, step - 1, i],
+                source, target.at[step - 1], send_sem.at[part, stage - 1, step - 1, i], recv_sem.at[part, stage - 1, step - 1, i],
                 device_id=device(to, core), device_id_type=MESH)
             for i, (source, target) in enumerate(zip(sources, targets))
         ]
@@ -506,30 +523,57 @@
             sides[pair + i] = jnp.concatenate([top, total, scale, scale], axis=0)
         target_side[...] = jnp.concatenate(sides, axis=0)
 
-    keep = [[pltpu.make_async_copy(source, target, own_sem.at[part, i])
-             for i, (source, target) in enumerate(zip(cut(part, place[part]), buffers[part][:2]))] for part in range(3)]
-    for pair in keep:
-        for copy in pair:
+    def keep(part):
+        p0, p0s, _, _, near, nears = buffers[part][:6]
+        moves = list(zip(cut(part, place[part]), (p0, p0s)))
+        for way in range(2):
+            moves += zip(cut(part, along(place, part, (1, 3)[way])[part], way), (near.at[way], nears.at[way]))
+        return [pltpu.make_async_copy(source, target, own_sem.at[part, i]) for i, (source, target) in enumerate(moves)]
+
+    for part in range(3):
+        for copy in keep(part):
             copy.start()
     greet(place, core)
-    for part in range(3):
-        start(part, 0)
-    for part in range(3):
-        p0, p0s, r1, r1s, m1, m1s = buffers[part][:6]
-        for copy in keep[part]:
+    for kind in range(2):
+        for part in range(3):
+            for way in range(2):
+                for copy in ring(part, way, kind):
+                    copy.start()
+    for part in range(3):
+        near, nears, rin, rins, rout, routs = buffers[part][4:10]
+        for copy in keep(part):
             copy.wait()
-        arrive(part, 0)
+        for way in range(2):
+            for copy in ring(part, way, 0):
+                copy.wait_recv()
+
+            def passing(n, _):
+                i, j = n // 4, n % 4
+                fold(part, [(near.at[way, i, j], nears.at[way, i, j]), (rin.at[way, i, j], rins.at[way, i, j])],
+                     rout.at[way, i, j], routs.at[way, i, j])
+                return 0
+
+            lax.fori_loop(0, 8, passing, 0, unroll=4)
+            for copy in ring(part, way, 2):
+                copy.start()
+    for part in range(3):
+        p0, p0s, r1, r1s = buffers[part][:4]
+        m1, m1s = buffers[part][10:12]
+        for way in range(2):
+            for kind in (1, 2):
+                for copy in ring(part, way, kind):
+                    copy.wait_recv()
 
         def first(n, _):
             i, j = n // 4, n % 4
-            fold(part, [(p0.at[i, j], p0s.at[i, j])] + [(r1.at[k, i, j], r1s.at[k, i, j]) for k in range(3)],
+            fold(part, [(p0.at[i, j], p0s.at[i, j])] + [(r1.at[k, i, j], r1s.at[k, i, j]) for k in range(2)],
                  m1.at[i, j], m1s.at[i, j])
             return 0
 
-        lax.fori_loop(0, 16, first, 0)
+        lax.fori_loop(0, 16, first, 0, unroll=4)
         start(part, 1)
     for part in range(3):
-        m1, m1s, r2, r2s, m2, m2s = buffers[part][4:10]
+        m1, m1s, r2, r2s, m2, m2s = buffers[part][10:16]
         at = place[(part + 1) % 3]
         arrive(part, 1)
 
@@ -538,11 +582,11 @@
                  m2.at[c], m2s.at[c])
             return 0
 
-        lax.fori_loop(0, 4, second, 0)
+        lax.fori_loop(0, 4, second, 0, unroll=4)
         start(part, 2)
     pieces = [[], []]
     for part in range(3):
-        m2, m2s, r3, r3s = buffers[part][8:]
+        m2, m2s, r3, r3s = buffers[part][14:]
         at = place[(part + 2) % 3]
         arrive(part, 2)
         sources = [(m2.at[at], m2s.at[at])] + [(r3.at[k], r3s.at[k]) for k in range(3)]
@@ -567,7 +611,11 @@
     out_ref[...] = wide[...].astype(jnp.bfloat16)
 
     for part in range(3):
-        for stage in range(3):
+        for way in range(2):
+            for kind in range(3):
+                for copy in ring(part, way, kind):
+                    copy.wait_send()
+        for stage in (1, 2):
             for step in (1, 2, 3):
                 for copy in copies(part, stage, step):
                     copy.wait_send()
@@ -578,7 +626,7 @@
     dma = pltpu.SemaphoreType.DMA
     buffers = []
     for _, pairs, _, many in SPLIT:
-        for lead in ((4, 4), (3, 4, 4), (4, 4), (3, 4), (4,), (3,)):
+        for lead in ((4, 4), (2, 4, 4), (2, 2, 4), (2, 2, 4), (2, 2, 4), (4, 4), (3, 4), (4,), (3,)):
             buffers += [pltpu.VMEM((*lead, pairs, many, 128), jnp.int16), pltpu.VMEM((*lead, 8, 128), jnp.float32)]
     return pl.pallas_call(
         merge_kernel,
@@ -588,7 +636,7 @@
         scratch_shapes=[
             *buffers,
             pltpu.VMEM((2, 4, 32, 128), jnp.float32), pltpu.VMEM((4, 32, 128), jnp.float32), pltpu.VMEM((4, 64, 128), jnp.float32),
-            dma((3, 3, 3, 2)), dma((3, 3, 3, 2)), dma((3, 2)), dma((2,)),
+            dma((3, 2, 3, 2)), dma((3, 2, 3, 2)), dma((3, 2, 3, 2)), dma((3, 2, 3, 2)), dma((3, 6)), dma((2,)),
         ],
         compiler_params=pltpu.CompilerParams(collective_id=1, has_side_effects=True, vmem_limit_bytes=62 * 2**20),
         name="merge_parts",

time: 135 us -> 129 us (0.956)
  Pallas kernels: 133 us -> 126 us
    pallas_call x1, Pallas kernels: 55.7 us -> 42 us  [merge_parts(): pl.pallas_call(merge_kernel, out_shape=jax.ShapeDtypeStruct((4, 64, 128),...]
    pallas_call x1, Pallas kernels: 39.3 us -> 46.4 us  [attend(): pl.pallas_call(attend_kernel, grid=(2,), in_specs=[pl.BlockSpec(memory_sp...]
where the time goes in v5:
time: 129 us; the launch traced here: 128 us
  Pallas kernels  126 us (98%)
  local copies, waits for them, and re-layouts  1.47 us (1%)
    pallas_call x1, Pallas kernels, attend(): pl.pallas_call(attend_kernel, grid=(2,), in_specs=[pl.BlockSpec(memory_sp...  46.4 us
    pallas_call x1, Pallas kernels, merge_parts(): pl.pallas_call(merge_kernel, out_shape=jax.ShapeDtypeStruct((4, 64, 128),...  42 us
    pallas_call x1, Pallas kernels, gather_queries(): pl.pallas_call(gather_kernel, out_shape=[jax.ShapeDtypeStruct((4, 4, 4, 2...  38 us

profile of v5, /device:TPU:1, one launch (start us, length us, event | category | flops | bytes accessed | tf_op | source)
XLA Modules:
  0.0 127.9 jit_solution(5155876433238927147)
XLA Ops:
  0.0 38.0 %gather_queries.1 = (bf16[4,4,4,256,128]{4,3,2,1,0:T(8,128)(2,1)}, s32[4,8,128]{2,1,0:T(8,128)}, bf16[18,4,256,128]{3,2,1,0:T(8,128)(2,1)}, bf16[18,4,128,256]{3,2,1,0:T(8,128)(2,1)}, s32[8,128]{1,0:T(8,128)}) custom-call(bf16[4,64,128]{2,1,0:T(8,128)(2,1)} %q_ref.1, s32[8]{0:T(128)} %bitcast.15, s32[8]{0:T(128)} %slot_ref.1, s32[8]{0:T(128)} %valid_ref.1, ...), custom_call_target="tpu_custom_call" | custom-call | tf_op jit(solution)/shard_map/gather_queries/pallas_call | solution.py:261
  38.0 46.4 %attend.1 = (s16[64,2,128,128]{3,2,1,0:T(8,128)(2,1)}, f32[64,8,128]{2,1,0:T(8,128)}) custom-call(s32[4,8,128]{2,1,0:T(8,128)} %get-tuple-element.12.list_ref, s32[8,128]{1,0:T(8,128)} %get-tuple-element.13.plan_ref, bf16[64,256,128]{2,1,0:T(8,128)(2,1)} %bitcast.10, bf16[18,4,256,128]{3,2,1,0:T(8,128)(2,1)} %get-tuple-element.15.pk_ref, ...), custom_call_target="tpu_custom_call" | custom-call | tf_op jit(solution)/shard_map/attend/pallas_call | solution.py:420
  84.4 42.0 %merge_parts.1 = bf16[4,64,128]{2,1,0:T(8,128)(2,1)} custom-call(s16[4,4,4,2,128,128]{5,4,3,2,1,0:T(8,128)(2,1)} %bitcast.11, f32[4,4,4,8,128]{4,3,2,1,0:T(8,128)} %bitcast.12), custom_call_target="tpu_custom_call" | custom-call | tf_op jit(solution)/shard_map/merge_parts/pallas_call | solution.py:631
  126.4 1.5 %copy.10 = bf16[4,64,128]{2,1,0:T(8,128)(2,1)} copy(bf16[4,64,128]{2,1,0:T(8,128)(2,1)} %merge_parts.1) | data formatting | bytes 131072

commit v6 on v5

--- a/solution.py
+++ b/solution.py
@@ -14,7 +14,7 @@
 NN = (((1,), (0,)), ((), ()))
 MESH = pl.DeviceIdType.MESH
 PARTS = ((0, 48, 48), (96, 32, 32), (160, 48, 48))
-SPLIT = ((0, 1, 0, 80), (1, 1, 0, 80), (0, 2, 80, 48))
+SPLIT = ((0, 1, 0, 96), (1, 1, 0, 96), (0, 2, 96, 32))
 ORDERS = ((0, 1, 2), (1, 2, 0), (0, 2, 1))
 JOBS = 14
 COSTS = (115, 90, 72)
@@ -170,6 +170,8 @@
         copies = []
         for i in which:
             half, step, origin = plan[i]
+            if phase == 0 and i > 3:
+                step, origin = 2, 0
             source = along(place, axis, origin)
             where = [slice(None) if d in order[:phase] else source[d] for d in range(3)]
             block = all_ref.at[where[0], where[1], where[2], halves[half]]
@@ -223,13 +225,14 @@
                     links(part, phase - 1, (i,))[0].wait_recv()
             if phase == 1 and part == 0:
                 keep.wait()
-            for copy in links(part, phase, range(4)):
+            for copy in links(part, phase, range(4 if phase else 6)):
                 copy.start()
         over(*((0, 0), (2, 4), (6, 10))[phase], regroup)
         for part in range(3):
             for i in (0, 1):
                 links(part, phase, (i,))[0].wait_recv()
-                links(part, phase, (i + 4,))[0].start()
+                if phase:
+                    links(part, phase, (i + 4,))[0].start()
         if phase == 0:
             balance()
         over(*((0, 2), (4, 6), (10, 16))[phase], regroup)
@@ -327,21 +330,22 @@
             v = jnp.transpose(jnp.concatenate([v, jnp.zeros((120, 128), jnp.float32)], axis=0))
             sv_ref[g] = jnp.concatenate([v, ones], axis=0).astype(jnp.bfloat16)
 
-        def fix(n, _):
-            slot, valid = jobs[0, n], jobs[1, n]
-            pltpu.make_async_copy(pk_ref.at[slot], kj.at[n], sem.at[0, n]).wait()
-            pltpu.make_async_copy(pv_ref.at[slot], vj.at[n, :, 0:128], sem.at[1, n]).wait()
-            live_row = lax.broadcasted_iota(jnp.int32, (256, 128), 0) < valid
-            live_lane = lax.broadcasted_iota(jnp.int32, (128, 256), 1) < valid
+    def fix(n, _):
+        slot, valid = jobs[0, n], jobs[1, n]
+        pltpu.make_async_copy(pk_ref.at[slot], kj.at[n], sem.at[0, n]).wait()
+        pltpu.make_async_copy(pv_ref.at[slot], vj.at[n, :, 0:128], sem.at[1, n]).wait()
+        live_row = lax.broadcasted_iota(jnp.int32, (256, 128), 0) < valid
+        live_lane = lax.broadcasted_iota(jnp.int32, (128, 256), 1) < valid
+        for g in range(4):
+            vj[n, g, 128:144] = live_lane[0:16].astype(jnp.float32).astype(jnp.bfloat16)
+
+        @pl.when(valid < 256)
+        def _():
             for g in range(4):
                 keys = kj[n, g].astype(jnp.float32)
                 kj[n, g] = jnp.where(live_row, keys, keys[0:1]).astype(jnp.bfloat16)
                 vj[n, g, 0:128] = jnp.where(live_lane, vj[n, g, 0:128].astype(jnp.float32), 0.0).astype(jnp.bfloat16)
-                vj[n, g, 128:144] = live_lane[0:16].astype(jnp.float32).astype(jnp.bfloat16)
-            return 0
-
-        for i in range(3):
-            lax.fori_loop(starts(i), starts(i) + count[i], fix, 0)
+        return 0
 
     pair = pl.program_id(0)
     suffix_at = (lax.axis_index("store") * 16 + lax.axis_index("ctx")) * 8
@@ -357,6 +361,12 @@
         w = jnp.concatenate([w, jnp.zeros((120, 4096), jnp.float32)], axis=0).astype(jnp.bfloat16)
         acc[half] = matmul(sv_ref[pair * 2 + half], w)
         peak[half] = t
+
+        if half == 0:
+            @pl.when(pair == 0)
+            def _():
+                for i in range(3):
+                    lax.fori_loop(starts(i), starts(i) + count[i], fix, 0)
 
         def unit(first, number, keys):
             stack = kj[pl.ds(first, number), pair * 2 + half, 0:keys, :].reshape(number * keys, 128)
@@ -403,10 +413,10 @@
                 top = jnp.where(low, pa, pltpu.roll(jnp.broadcast_to(pb, (8, 128)), 64, 1)[0:1])
             values, scale = encode(whole[0:128])
             o_ref[i * 2 + odd, 0] = values
-            side_ref[i * 2 + odd, pl.ds(pair * 4, 4), :] = jnp.concatenate([top, whole[128:129], scale, scale], axis=0)
+            side_ref[i * 2 + odd, 0] = jnp.concatenate([top, whole[128:129], scale, scale], axis=0)
         return 0
 
-    lax.fori_loop(0, 32, emit, 0, unroll=8)
+    lax.fori_loop(0, 32, emit, 0, unroll=16)
 
 
 def encode(x):
@@ -428,8 +438,8 @@
             pl.BlockSpec((32, 128), lambda i: (0, 0)),
             pl.BlockSpec((32, 128), lambda i: (0, 0)),
         ],
-        out_specs=[pl.BlockSpec((64, 1, 128, 128), lambda i: (0, i, 0, 0)), pl.BlockSpec((64, 8, 128), lambda i: (0, 0, 0))],
-        out_shape=[jax.ShapeDtypeStruct((64, 2, 128, 128), jnp.int16), jax.ShapeDtypeStruct((64, 8, 128), jnp.float32)],
+        out_specs=[pl.BlockSpec((64, 1, 128, 128), lambda i: (0, i, 0, 0)), pl.BlockSpec((64, 1, 4, 128), lambda i: (0, i, 0, 0))],
+        out_shape=[jax.ShapeDtypeStruct((64, 2, 128, 128), jnp.int16), jax.ShapeDtypeStruct((64, 2, 4, 128), jnp.float32)],
         scratch_shapes=[
             pltpu.VMEM((2 * JOBS, 4, 256, 128), jnp.bfloat16), pltpu.VMEM((2 * JOBS, 4, 144, 256), jnp.bfloat16),
             pltpu.VMEM((4, 16, 128), jnp.bfloat16), pltpu.VMEM((4, 144, 128), jnp.bfloat16), pltpu.VMEM((2, 32, 128), jnp.float32),
@@ -463,7 +473,7 @@
         if half is not None:
             where[1 if part == 0 else 0] = pl.ds(half * 2, 2)
         return (o_ref.at[where[0], where[1], where[2], pl.ds(pair, pairs), pl.ds(row, many)],
-                side_ref.at[where[0], where[1], where[2]])
+                side_ref.at[where[0], where[1], where[2], pl.ds(pair, pairs)])
 
     def line(part, ref, at, other=slice(None)):
         return ref.at[other, at] if part == 1 else ref.at[at, other]
@@ -511,17 +521,13 @@
                 copy.wait_recv()
 
     def combine(part, sources):
-        pair, pairs = SPLIT[part][:2]
-        return [merge([(values[i], side[(pair + i) * 4:(pair + i) * 4 + 4]) for values, side in sources]) for i in range(pairs)]
+        return [merge([(values[i], side[i]) for values, side in sources]) for i in range(SPLIT[part][1])]
 
     def fold(part, sources, target, target_side):
-        pair = SPLIT[part][0]
-        sides = [jnp.zeros((4, 128), jnp.float32)] * 2
         for i, (weighted, top, total) in enumerate(combine(part, sources)):
             values, scale = encode(weighted)
             target[i] = values
-            sides[pair + i] = jnp.concatenate([top, total, scale, scale], axis=0)
-        target_side[...] = jnp.concatenate(sides, axis=0)
+            target_side[i] = jnp.concatenate([top, total, scale, scale], axis=0)
 
     def keep(part):
         p0, p0s, _, _, near, nears = buffers[part][:6]
@@ -627,7 +633,7 @@
     buffers = []
     for _, pairs, _, many in SPLIT:
         for lead in ((4, 4), (2, 4, 4), (2, 2, 4), (2, 2, 4), (2, 2, 4), (4, 4), (3, 4), (4,), (3,)):
-            buffers += [pltpu.VMEM((*lead, pairs, many, 128), jnp.int16), pltpu.VMEM((*lead, 8, 128), jnp.float32)]
+            buffers += [pltpu.VMEM((*lead, pairs, many, 128), jnp.int16), pltpu.VMEM((*lead, pairs, 4, 128), jnp.float32)]
     return pl.pallas_call(
         merge_kernel,
         out_shape=jax.ShapeDtypeStruct((4, 64, 128), jnp.bfloat16),
@@ -640,7 +646,7 @@
         ],
         compiler_params=pltpu.CompilerParams(collective_id=1, has_side_effects=True, vmem_limit_bytes=62 * 2**20),
         name="merge_parts",
-    )(values.reshape(4, 4, 4, 2, 128, 128), side.reshape(4, 4, 4, 8, 128))
+    )(values.reshape(4, 4, 4, 2, 128, 128), side.reshape(4, 4, 4, 2, 4, 128))
 
 
 def local(queries, suffix_k, suffix_v, pool_k, pool_v, list_holder, list_slot, list_valid):

time: 129 us -> 130 us (level); the launches traced: 128 us -> 132 us
  Pallas kernels: 126 us -> 130 us
    pallas_call x1, Pallas kernels: 42 us -> 61.8 us  [merge_parts(): pl.pallas_call(merge_kernel, out_shape=jax.ShapeDtypeStruct((4, 64, 128),...]
    pallas_call x1, Pallas kernels: 46.4 us -> 30.3 us  [attend(): pl.pallas_call(attend_kernel, grid=(2,), in_specs=[pl.BlockSpec(memory_sp...]
where the time goes in v6:
time: 130 us; the launch traced here: 132 us
  Pallas kernels  130 us (100%)
  local copies, waits for them, and re-layouts  1.47 us (1%)
    pallas_call x1, Pallas kernels, merge_parts(): pl.pallas_call(merge_kernel, out_shape=jax.ShapeDtypeStruct((4, 64, 128),...  61.8 us
    pallas_call x1, Pallas kernels, gather_queries(): pl.pallas_call(gather_kernel, out_shape=[jax.ShapeDtypeStruct((4, 4, 4, 2...  38.3 us
    pallas_call x1, Pallas kernels, attend(): pl.pallas_call(attend_kernel, grid=(2,), in_specs=[pl.BlockSpec(memory_sp...  30.3 us

profile of v6, /device:TPU:1, one launch (start us, length us, event | category | flops | bytes accessed | tf_op | source)
XLA Modules:
  0.0 132.0 jit_solution(7132562684526437871)
XLA Ops:
  0.0 38.3 %gather_queries.1 = (bf16[4,4,4,256,128]{4,3,2,1,0:T(8,128)(2,1)}, s32[4,8,128]{2,1,0:T(8,128)}, bf16[18,4,256,128]{3,2,1,0:T(8,128)(2,1)}, bf16[18,4,128,256]{3,2,1,0:T(8,128)(2,1)}, s32[8,128]{1,0:T(8,128)}) custom-call(bf16[4,64,128]{2,1,0:T(8,128)(2,1)} %q_ref.1, s32[8]{0:T(128)} %bitcast.15, s32[8]{0:T(128)} %slot_ref.1, s32[8]{0:T(128)} %valid_ref.1, ...), custom_call_target="tpu_custom_call" | custom-call | tf_op jit(solution)/shard_map/gather_queries/pallas_call | solution.py:264
  38.3 30.3 %attend.1 = (s16[64,2,128,128]{3,2,1,0:T(8,128)(2,1)}, f32[64,2,4,128]{3,2,1,0:T(4,128)}) custom-call(s32[4,8,128]{2,1,0:T(8,128)} %get-tuple-element.12.list_ref, s32[8,128]{1,0:T(8,128)} %get-tuple-element.13.plan_ref, bf16[64,256,128]{2,1,0:T(8,128)(2,1)} %bitcast.10, bf16[18,4,256,128]{3,2,1,0:T(8,128)(2,1)} %get-tuple-element.15.pk_ref, ...), custom_call_target="tpu_custom_call" | custom-call | tf_op jit(solution)/shard_map/attend/pallas_call | solution.py:430
  68.7 61.8 %merge_parts.1 = bf16[4,64,128]{2,1,0:T(8,128)(2,1)} custom-call(s16[4,4,4,2,128,128]{5,4,3,2,1,0:T(8,128)(2,1)} %bitcast.11, f32[4,4,4,2,4,128]{5,4,3,2,1,0:T(4,128)} %bitcast.12), custom_call_target="tpu_custom_call" | custom-call | tf_op jit(solution)/shard_map/merge_parts/pallas_call | solution.py:637
  130.5 1.5 %copy.10 = bf16[4,64,128]{2,1,0:T(8,128)(2,1)} copy(bf16[4,64,128]{2,1,0:T(8,128)(2,1)} %merge_parts.1) | data formatting | bytes 131072
